TPU v7x, 256 devices: a whole 4x4x8 slice. The times are simulated.
256 devices in a mesh: row: 64 (over x, y, z_lo), col: 4 (over z_hi, core).
Axes of the slice: x: 4, y: 4, z: 8 (z_hi: 2, z_lo: 4; z = z_hi * 4 + z_lo), core: 2. Of those that a mesh axis runs over, the one named last changes fastest.
Arguments:
- pair: bfloat16 [256, 256, 128], P('row', 'col'), may hold values from -6 to 6
- atoms: bfloat16 [8192, 128], P('row'), may hold values from -6 to 6
- atom_token: int32 [8192], P('row'), may hold values from 0 to 255, never falling along the last dimension, each value on 1 to 64 neighbouring positions
- tri_proj: bfloat16 [128, 640], replicated, may hold values from -0.5 to 0.5
- tri_out: bfloat16 [128, 128], replicated, may hold values from -0.5 to 0.5
- w_qkv: bfloat16 [128, 384], replicated, may hold values from -0.5 to 0.5
- w_attn_out: bfloat16 [128, 128], replicated, may hold values from -0.5 to 0.5
- w_token: bfloat16 [128, 384], replicated, may hold values from -0.5 to 0.5
- w_row: bfloat16 [384, 128], replicated, may hold values from -0.3125 to 0.3125
- w_col: bfloat16 [384, 128], replicated, may hold values from -0.3125 to 0.3125
Outputs:
- pair_out: bfloat16 [256, 256, 128], P('row', 'col')
- atom_out: bfloat16 [8192, 128], P('row')
Inputs may be any that keep to these rules, and one draw needn't show every extreme that they name: `atom_token`: never falling along atoms; each of the 256 tokens owns 1 to 64 consecutive atoms, one token exactly 64.
All inputs are finite; a program needn't handle non-finite values.
Results may differ from a plain program's by a relative error of at most 0.009.
Values may be sent and summed in bfloat16 or wider, within the bound.
A program may use at most 64 MiB of HBM per device.

v0:
```python
import jax
import jax.numpy as jnp
from jax import lax
from jax.sharding import PartitionSpec as P

HEADS = 4


def padded_2(cells, sides, width):
    for axis, dim in sides:
        count = lax.axis_size(axis)
        ends = count - 1
        head = lax.slice_in_dim(cells, 0, width, axis=dim)
        tail = lax.slice_in_dim(cells, cells.shape[dim] - width, cells.shape[dim], axis=dim)
        cells = jnp.concatenate(
            [
                lax.ppermute(tail, axis, [(i, (i + 1) % count) for i in range(ends)]),
                cells,
                lax.ppermute(head, axis, [((i + 1) % count, i) for i in range(ends)]),
            ],
            axis=dim,
        )
    return cells


def layer_norm(values):
    mean = jnp.mean(values, axis=-1, keepdims=True)
    centered = values - mean
    variance = jnp.mean(centered * centered, axis=-1, keepdims=True)
    return centered / jnp.sqrt(variance + 1e-05)


def window_attend(queries, keys, values, offset, total):
    count = queries.shape[0] // 32
    width = queries.shape[1]
    query_blocks = queries.reshape(count, 32, HEADS, width // HEADS)
    key_blocks = keys.reshape(count + 3, 32, width)
    value_blocks = values.reshape(count + 3, 32, width)
    key_win = jnp.concatenate([key_blocks[s : s + count] for s in range(4)], axis=1).reshape(
        count, 128, HEADS, width // HEADS
    )
    value_win = jnp.concatenate([value_blocks[s : s + count] for s in range(4)], axis=1).reshape(
        count, 128, HEADS, width // HEADS
    )
    scores = jnp.einsum(
        "wqhd,wkhd->whqk", query_blocks, key_win, preferred_element_type=jnp.float32
    ) * float(width // HEADS) ** (-0.5)
    position = (
        offset
        + 32 * jnp.arange(count, dtype=jnp.int32)[:, None]
        + jnp.arange(128, dtype=jnp.int32)[None, :]
        - 48
    )
    valid = (position >= 0) & (position < total)
    scores = jnp.where(valid[:, None, None, :], scores, -1e30)
    probs = jax.nn.softmax(scores, axis=-1).astype(jnp.bfloat16)
    attended = jnp.einsum("whqk,wkhd->wqhd", probs, value_win, preferred_element_type=jnp.float32)
    return attended.astype(jnp.bfloat16).reshape(count * 32, width)


def per_device(
    pair, atoms, atom_token, tri_proj, tri_out, w_qkv, w_attn_out, w_token, w_row, w_col
):
    rows_here, cols_here, width = pair.shape
    atoms_here, atom_width = atoms.shape
    row_count = lax.axis_size("row")
    tok_total = rows_here * row_count
    row_index = lax.axis_index("row")
    col_index = lax.axis_index("col")
    atom_norm = layer_norm(atoms.astype(jnp.float32)).astype(jnp.bfloat16)
    padded = padded_2(atom_norm, (("row", 0),), 48)
    qkv = jnp.dot(padded, w_qkv, preferred_element_type=jnp.float32).astype(jnp.bfloat16)
    queries = qkv[48 : 48 + atoms_here, :atom_width]
    attended = window_attend(
        queries,
        qkv[:, atom_width : 2 * atom_width],
        qkv[:, 2 * atom_width :],
        row_index * atoms_here,
        atoms_here * row_count,
    )
    atom_out = (
        atoms.astype(jnp.float32)
        + jnp.dot(attended, w_attn_out, preferred_element_type=jnp.float32)
    ).astype(jnp.bfloat16)
    hidden = jax.nn.relu(jnp.dot(atom_out, w_token, preferred_element_type=jnp.float32))
    onehot = (atom_token[:, None] == jnp.arange(tok_total, dtype=jnp.int32)[None, :]).astype(
        jnp.float32
    )
    partial_sum = lax.dot_general(
        onehot,
        hidden,
        (((0,), (0,)), ((), ())),
        precision=lax.Precision.HIGHEST,
        preferred_element_type=jnp.float32,
    )
    partial_count = jnp.sum(onehot, axis=0)
    token_sum, token_count = lax.psum((partial_sum, partial_count), "row")
    single = (token_sum / token_count[:, None]).astype(jnp.bfloat16)
    row_single = lax.dynamic_slice_in_dim(single, row_index * rows_here, rows_here, 0)
    col_single = lax.dynamic_slice_in_dim(single, col_index * cols_here, cols_here, 0)
    pair_norm = layer_norm(pair.astype(jnp.float32)).astype(jnp.bfloat16)
    proj = jnp.dot(
        pair_norm.reshape(rows_here * cols_here, width),
        tri_proj,
        preferred_element_type=jnp.float32,
    ).reshape(rows_here, cols_here, 5 * width)
    left = (jax.nn.sigmoid(proj[..., :width]) * proj[..., width : 2 * width]).astype(jnp.bfloat16)
    right = (
        jax.nn.sigmoid(proj[..., 2 * width : 3 * width]) * proj[..., 3 * width : 4 * width]
    ).astype(jnp.bfloat16)
    gate = jax.nn.sigmoid(proj[..., 4 * width :])
    left_whole = lax.all_gather(left, "col", axis=1, tiled=True)
    right_gathered = lax.all_gather(right, "row", axis=0, tiled=True)
    right_mine = lax.all_to_all(right_gathered, "col", split_axis=0, concat_axis=1, tiled=True)
    tri = jnp.einsum("ikc,jkc->ijc", left_whole, right_mine, preferred_element_type=jnp.float32)
    tri_norm = layer_norm(tri).astype(jnp.bfloat16)
    update = gate * jnp.dot(
        tri_norm.reshape(rows_here * cols_here, width), tri_out, preferred_element_type=jnp.float32
    ).reshape(rows_here, cols_here, width)
    rows_term = jnp.dot(row_single, w_row, preferred_element_type=jnp.float32)
    cols_term = jnp.dot(col_single, w_col, preferred_element_type=jnp.float32)
    pair_out = (
        pair.astype(jnp.float32) + update + rows_term[:, None, :] + cols_term[None, :, :]
    ).astype(jnp.bfloat16)
    return (pair_out, atom_out)


def solution(mesh):
    return jax.shard_map(
        per_device,
        mesh=mesh,
        in_specs=(
            P("row", "col", None),
            P("row", None),
            P("row"),
            P(),
            P(),
            P(),
            P(),
            P(),
            P(),
            P(),
        ),
        out_specs=(P("row", "col", None), P("row", None)),
        check_vma=False,
    )
```

profile of v0, /device:TPU:128, one launch (start us, length us, event | category | flops | bytes accessed | tf_op | source)
XLA Modules:
  0.0 1179.7 jit_solution(14620331105762861438)
XLA Ops:
  7.2 1.0 convert_reduce_fusion
  8.2 1.0 fusion.14
  9.3 1.1 fusion.10
  10.4 0.7 fusion.16
  11.2 358.0 %all-gather.2.cloned.1.call-done = bf16[256,64,128]{2,1,0:T(8,128)(2,1)} async-done(((bf16[4,64,128]{2,1,0:T(8,128)(2,1)}), bf16[256,64,128]{2,1,0:T(8,128)(2,1)}) %all-gather.2.cloned.1.call-update) | async-done | bytes 4194320 | tf_op jit(solution)/shard_map/all_gather | solution.py:113
  369.1 7.4 all-to-all-start
  376.7 0.2 fusion.48
  377.0 1.3 collective-permute-start.1
  378.3 4.5 collective-permute-start
  383.0 82.3 %collective-permute-done.1 = bf16[48,128]{1,0:T(8,128)(2,1)S(1)} collective-permute-done((bf16[48,128]{1,0:T(8,128)(2,1)S(1)}, bf16[48,128]{1,0:T(8,128)(2,1)S(1)}, u32[]{:S(2)}, u32[]{:S(2)}) %collective-permute-start.1) | collective-permute-done | bytes 12320 | tf_op jit(solution)/shard_map/ppermute | solution.py:19
  465.3 1.7 collective-permute-done
  467.0 0.2 convolution_convert_fusion
  467.6 0.1 copy.71
  468.1 0.1 copy.69
  469.5 0.5 fusion.83
  469.9 0.3 fusion.2
  470.2 1.1 fusion.4
  471.4 0.1 copy.78
  471.8 0.2 convolution_maximum_fusion
  472.0 1.2 fusion.44
  473.3 9.7 all_gather.7
  483.0 0.2 copy.67
  483.3 186.0 %psum.15 = f32[256]{0:T(256)S(1)} all-reduce(f32[256]{0:T(256)S(1)} %convert_reduce_fusion.1), channel_id=1, replica_groups=mesh['row'=64,'col'=4] {'row'}, use_global_device_ids=true, to_apply=%region_10.11 | all-reduce | flops 256 | bytes 2048 | tf_op jit(solution)/shard_map/psum | solution.py:97
  669.3 485.2 %all-reduce.2.cloned.1.call-done = f32[256,384]{1,0:T(8,128)} async-done(((f32[256,384]{1,0:T(8,128)}), f32[256,384]{1,0:T(8,128)}) %all-reduce.2.cloned.1.call-update) | async-done | bytes 393232 | tf_op jit(solution)/shard_map/psum | solution.py:97
  1154.5 1.1 divide_convert_fusion
  1155.6 0.1 fusion.65
  1155.8 0.1 fusion.58
  1155.9 5.6 copy.65
  1161.5 6.8 copy.66
  1168.3 3.4 fusion.82
  1171.7 0.2 multiply_reduce_fusion
  1172.0 0.8 fusion.8
  (58 shorter events, 2.8 us)
Async XLA Ops:
  7.2 2.1 copy-start
  7.2 362.0 %all-gather.2.cloned.1.call-start = ((), (), s32[]{:S(2)}) async-start(), calls=%async_computation.1 | async-start | bytes 4259840 | tf_op jit(solution)/shard_map/all_gather | solution.py:113
  11.2 365.4 %copy-start.2 = (bf16[128,128]{1,0:T(8,128)(2,1)S(1)}, bf16[128,128]{1,0:T(8,128)(2,1)}, u32[]{:S(2)}) copy-start(bf16[128,128]{1,0:T(8,128)(2,1)} %param.11) | copy-start | bytes 98308
  11.2 455.8 %copy-start.5 = (bf16[128,384]{1,0:T(8,128)(2,1)S(1)}, bf16[128,384]{1,0:T(8,128)(2,1)}, u32[]{:S(2)}) copy-start(bf16[128,384]{1,0:T(8,128)(2,1)} %param.15) | copy-start | bytes 294916
  369.1 786.8 %all-to-all-start = ((bf16[256,64,128]{2,1,0:T(8,128)(2,1)}), bf16[256,64,128]{2,1,0:T(8,128)(2,1)}, u32[]{:S(2)}, u32[]{:S(2)}) async-start(bf16[256,64,128]{2,1,0:T(8,128)(2,1)} %all-gather.2.cloned.1.call-done), calls=%async_computation | async-start | bytes 8388608 | tf_op jit(solution)/shard_map/all_to_all | solution.py:114
  376.6 777.9 %all-reduce.2.cloned.1.call-start = ((), (), s32[]{:S(2)}) async-start(), calls=%async_computation.2 | async-start | bytes 786432 | tf_op jit(solution)/shard_map/psum | solution.py:97
  377.0 88.2 %collective-permute-start.1 = (bf16[48,128]{1,0:T(8,128)(2,1)S(1)}, bf16[48,128]{1,0:T(8,128)(2,1)S(1)}, u32[]{:S(2)}, u32[]{:S(2)}) collective-permute-start(bf16[48,128]{1,0:T(8,128)(2,1)S(1)} %get-tuple-element.14), channel_id=1, source_target_pairs={{4,0},{8,4},{12,8},{16,12},{20,16},{24,20},{28,24},{32,28},{36,32}... | collective-permute-start | bytes 36872 | tf_op jit(solution)/shard_map/ppermute | solution.py:19
  378.3 88.6 %collective-permute-start = (bf16[48,128]{1,0:T(8,128)(2,1)S(1)}, bf16[48,128]{1,0:T(8,128)(2,1)S(1)}, u32[]{:S(2)}, u32[]{:S(2)}) collective-permute-start(bf16[48,128]{1,0:T(8,128)(2,1)S(1)} %get-tuple-element.13), channel_id=1, source_target_pairs={{0,4},{4,8},{8,12},{12,16},{16,20},{20,24},{24,28},{28,32},{32,36}... | collective-permute-start | bytes 36872 | tf_op jit(solution)/shard_map/ppermute | solution.py:17
  383.0 88.7 %copy-start.8 = (bf16[128,128]{1,0:T(8,128)(2,1)S(1)}, bf16[128,128]{1,0:T(8,128)(2,1)}, u32[]{:S(2)}) copy-start(bf16[128,128]{1,0:T(8,128)(2,1)} %param.16) | copy-start | bytes 98308
  467.2 4.7 copy-start.6
  467.2 4.8 copy-start.9
  468.5 687.1 %copy-start.4 = (bf16[384,128]{1,0:T(8,128)(2,1)S(1)}, bf16[384,128]{1,0:T(8,128)(2,1)}, u32[]{:S(2)}) copy-start(bf16[384,128]{1,0:T(8,128)(2,1)} %param.18) | copy-start | bytes 294916
  468.5 687.2 %copy-start.7 = (bf16[384,128]{1,0:T(8,128)(2,1)S(1)}, bf16[384,128]{1,0:T(8,128)(2,1)}, u32[]{:S(2)}) copy-start(bf16[384,128]{1,0:T(8,128)(2,1)} %param.19) | copy-start | bytes 294916
  471.8 689.7 %copy-start.3 = (bf16[128,128]{1,0:T(8,128)(2,1)}, bf16[128,128]{1,0:T(8,128)(2,1)S(1)}, u32[]{:S(2)}) copy-start(bf16[128,128]{1,0:T(8,128)(2,1)S(1)} %fusion.9) | copy-start | bytes 98308
  1168.3 3.7 copy-start.1
  1168.3 3.7 copy-start.10
Sparse Core Ops, SparseCore 0:
  11.3 357.8 all-gather.1
  473.4 681.0 all-reduce.1
where the time goes:
time: 1180 us
  waiting for transfers between devices  927 us (79%)
  blocking collectives  196 us (17%)
  local copies, waits for them, and re-layouts  15 us (1%)
  between operations  14.4 us (1%)
  starting transfers between devices  13.3 us (1%)
    psum x1, waiting for transfers between devices, per_device(): token_sum, token_count = lax.psum((partial_sum, partial_count), 'row')  485 us
    all_gather x1, waiting for transfers between devices, per_device(): right_gathered = lax.all_gather(right, 'row', axis=0, tiled=True)  358 us
    psum x1, blocking collectives, per_device(): token_sum, token_count = lax.psum((partial_sum, partial_count), 'row')  186 us
    ppermute x1, waiting for transfers between devices, padded_2(): lax.ppermute(head, axis, [((i + 1) % count, i) for i in range(ends)])  82.3 us
  transfers between devices with their start and end apart: 5, of which 4 were waited for; matrix products, arithmetic and copies ran while one was open for 1% of the time, Pallas kernels for 0%

commit v1 on v0

v1 whole, which is shorter than its diff:
```python
import functools

import jax
import jax.numpy as jnp
from jax import lax
from jax.experimental import pallas as pl
from jax.experimental.pallas import tpu as pltpu
from jax.sharding import PartitionSpec as P

MESH = pl.DeviceIdType.MESH
F32 = jnp.float32
BF16 = jnp.bfloat16
HEADS = 4
C = 128


def normed(values):
    mean = jnp.mean(values, axis=-1, keepdims=True)
    centered = values - mean
    variance = jnp.mean(centered * centered, axis=-1, keepdims=True)
    return centered * lax.rsqrt(variance + 1e-05)


def sigmoid(values):
    return 0.5 * jnp.tanh(0.5 * values) + 0.5


def dot(a, b):
    return jnp.dot(a, b, preferred_element_type=F32)


def dot_nt(a, b):
    return lax.dot_general(a, b, (((1,), (1,)), ((), ())), preferred_element_type=F32)


def halves(low, high):
    lane = lax.broadcasted_iota(jnp.int32, low.shape, 1)
    even = jnp.where(lane < 64, low, pltpu.roll(high, 64, 1))
    odd = jnp.where(lane < 64, pltpu.roll(low, 64, 1), high)
    return even, odd


def kernel(
    pair_ref, atoms_ref, token_ref, tri_proj_ref, tri_out_ref, w_qkv_ref, w_attn_ref, w_token_ref,
    w_row_ref, w_col_ref, pair_out_ref, atom_out_ref,
    wide, send1, recv1, left, right, rights, send3, recv3, gate_ref, upd_ref,
    before, after, tok_send, tok_recv, x_send, x_recv, tot_ref, k_send, k_recv, r_send, r_recv,
    s_halo, r_halo, s_1, r_1, s_2, r_2, s_l, r_l, s_3, r_3, s_t, r_t, s_x, r_x, s_k, r_k, s_r, r_r,
):
    row, col = lax.axis_index("row"), lax.axis_index("col")
    x, p = row // 16, row % 16
    y, z_lo = p // 4, p % 4
    z_hi, core = col // 2, col % 2
    z = z_hi * 4 + z_lo
    group = z_hi * 16 + p
    parity = x % 2

    def plane(g):
        return (x * 16 + g % 16, 2 * (g // 16) + core)

    def next_row():
        carry_y = (z_lo + 1) // 4
        carry_x = (y + carry_y) // 4
        z_to = (z + 1) % 8
        row_to = ((x + carry_x) % 4) * 16 + ((y + carry_y) % 4) * 4 + z_to % 4
        return (row_to, 2 * (z_to // 4) + core)

    def prev_row():
        carry_y = (4 - z_lo) // 4
        carry_x = (3 - y + carry_y) // 4
        z_to = (z + 7) % 8
        row_to = ((x + 4 - carry_x) % 4) * 16 + ((y + 4 - carry_y) % 4) * 4 + z_to % 4
        return (row_to, 2 * (z_to // 4) + core)

    def along_x(step, core_to):
        return (((x + step) % 4) * 16 + p, 2 * z_hi + core_to)

    def token_peer(t):
        z_to = (z + 7 + (t % 4 + 9 - z) % 4) % 8
        return (x * 16 + (t // 4) * 4 + z_to % 4, 2 * (z_to // 4) + core)

    mate = (row, 2 * z_hi + 1 - core)
    flipped = (col * 16 + p, x)
    diagonal = x == col
    own_right = parity == core

    def remote(src, dst, send_sem, recv_sem, to):
        return pltpu.make_async_remote_copy(
            src_ref=src, dst_ref=dst, send_sem=send_sem, recv_sem=recv_sem, device_id=to, device_id_type=MESH
        )

    barrier = pltpu.get_barrier_semaphore()

    def hello(to):
        pl.semaphore_signal(barrier, inc=1, device_id=to, device_id_type=MESH)

    hello(next_row())
    hello(prev_row())

    @pl.loop(1, 32)
    def _(step):
        hello(plane((group + step) % 32))

    @pl.loop(1, 4)
    def _(step):
        hello(along_x(step, 0))
        hello(along_x(step, 1))

    hello(mate)

    @pl.when(jnp.logical_not(diagonal))
    def _():
        hello(flipped)

    pair_norm = normed(pair_ref[...].reshape(256, C).astype(F32)).astype(BF16)
    for side in range(2):
        at = 2 * side * C
        gated = sigmoid(dot(pair_norm, tri_proj_ref[:, at : at + C])) * dot(
            pair_norm, tri_proj_ref[:, at + C : at + 2 * C]
        )
        for half in range(2):
            flat = gated[half * 128 : half * 128 + 128].T
            for slot in range(4):
                wide[pl.ds(side * 8 + slot * 2 + half, 32, stride=16), :] = flat[slot * 32 : slot * 32 + 32]
    send1[...] = wide[...].reshape(32, 16, C).astype(BF16)
    recv1[pl.ds(group, 1)] = send1[pl.ds(group, 1)]
    tot_ref[...] = jnp.ones_like(tot_ref)

    pl.semaphore_wait(barrier, 2 + 31 + 6 + 1 + jnp.where(diagonal, 0, 1))

    to_next = remote(atoms_ref.at[pl.ds(80, 48)], before, s_halo.at[0], r_halo.at[0], next_row())
    to_prev = remote(atoms_ref.at[pl.ds(0, 48)], after, s_halo.at[1], r_halo.at[1], prev_row())
    to_next.start()
    to_prev.start()

    @pl.loop(1, 32)
    def _(step):
        to = (group + step) % 32
        remote(send1.at[to], recv1.at[group], s_1, r_1, plane(to)).start()

    gate_ref[...] = sigmoid(dot(pair_norm, tri_proj_ref[:, 4 * C :]))

    to_next.wait_recv()
    to_prev.wait_recv()
    atoms = atoms_ref[...].astype(F32)
    padded = jnp.concatenate([before[...].astype(F32), atoms, after[...].astype(F32)], axis=0)
    atom_norm = normed(padded).astype(BF16)
    qkv = dot(atom_norm, w_qkv_ref[...]).astype(BF16)
    head_of = lax.broadcasted_iota(jnp.int32, (32, C), 1) // 32
    attended = []
    for window in range(4):
        at = 32 * window
        query = qkv[48 + at : 80 + at, :C]
        query = jnp.concatenate(
            [jnp.where(head_of == h, query, jnp.zeros_like(query)) for h in range(HEADS)], axis=0
        )
        scores = dot_nt(query, qkv[at : at + 128, C : 2 * C]) * (32.0**-0.5)
        position = row * 128 + at - 48 + lax.broadcasted_iota(jnp.int32, (128, 128), 1)
        scores = jnp.where((position >= 0) & (position < 8192), scores, -1e30)
        probs = jnp.exp(scores - jnp.max(scores, axis=-1, keepdims=True))
        probs = (probs / jnp.sum(probs, axis=-1, keepdims=True)).astype(BF16)
        mixed = dot(probs, qkv[at : at + 128, 2 * C :])
        result = mixed[0:32]
        for h in range(1, HEADS):
            result = jnp.where(head_of == h, mixed[32 * h : 32 * h + 32], result)
        attended.append(result)
    attended = jnp.concatenate(attended, axis=0).astype(BF16)
    atom_out = (atoms + dot(attended, w_attn_ref[...])).astype(BF16)
    atom_out_ref[...] = atom_out
    hidden = jnp.maximum(dot(atom_out, w_token_ref[...]), 0.0).astype(BF16)
    summed = jnp.concatenate(
        [hidden[:, :C], hidden[:, C : 2 * C], hidden[:, 2 * C :], jnp.ones((128, C), BF16)], axis=0
    )
    line = lax.broadcasted_iota(jnp.int32, (256, 128), 0)
    to = line // 16
    z_to = (z + 7 + (to % 4 + 9 - z) % 4) % 8
    token_id = 64 * (2 * (z_to // 4) + core) + 4 * to + line % 4
    mine = token_id == token_ref[...]
    part = (line // 4) % 4
    picked = jnp.concatenate(
        [jnp.where(mine & (part == k), 1.0, 0.0).astype(BF16) for k in range(4)], axis=1
    )
    tok_send[...] = dot(picked, summed).reshape(16, 16, C)
    tok_recv[pl.ds(p, 1)] = tok_send[pl.ds(p, 1)]

    @pl.loop(1, 16)
    def _(step):
        t = (p + step) % 16
        remote(tok_send.at[t], tok_recv.at[p], s_t, r_t, token_peer(t)).start()

    remote(send1.at[pl.ds(0, 31)], recv1.at[pl.ds(0, 31)], s_1, r_1, mate).wait_recv()
    wide[...] = recv1[...].reshape(512, C).astype(F32)
    for side in (1, 0):
        for slot in range(4):
            for half in range(2):
                at = side * 8 + slot * 2 + half
                even, odd = halves(
                    wide[pl.ds(at, 16, stride=16), :], wide[pl.ds(256 + at, 16, stride=16), :]
                )
                both = jnp.concatenate([even, odd], axis=0).astype(BF16)
                if side:
                    right[slot, half * 32 : half * 32 + 32, :] = both
                else:
                    left[core, slot, half * 32 : half * 32 + 32, :] = both
        if side:
            place = (x // 2) * 2 + core

            @pl.when(own_right)
            def _():
                rights[pl.ds(place, 1)] = right[...][None]

            @pl.when(jnp.logical_not(own_right))
            def _():
                remote(right, rights.at[place], s_2.at[0], r_2.at[place], along_x(0, parity)).start()

            for step in range(1, 4):
                remote(right, rights.at[place], s_2.at[step], r_2.at[place], along_x(step, parity)).start()
    to_mate = remote(left.at[core], left.at[core], s_l, r_l, mate)
    to_mate.start()

    remote(tok_send.at[pl.ds(0, 15)], tok_recv.at[pl.ds(0, 15)], s_t, r_t, mate).wait_recv()
    x_send[...] = jnp.sum(tok_recv[...], axis=0)
    x_recv[pl.ds(x, 1)] = x_send[...][None]
    for step in range(1, 4):
        remote(x_send, x_recv.at[x], s_x, r_x, along_x(step, core)).start()

    remote(left.at[1 - core], left.at[1 - core], s_l, r_l, mate).wait_recv()
    for place in range(4):

        @pl.when(jnp.logical_not(own_right & ((x // 2) * 2 + core == place)))
        def _():
            remote(right, rights.at[place], s_2.at[0], r_2.at[place], mate).wait_recv()

    for slot in range(4):
        tri = None
        for k in range(2):
            other = jnp.concatenate([rights[k, slot], rights[2 + k, slot]], axis=0)
            term = dot_nt(left[k, slot], other)
            tri = term if tri is None else tri + term
        for half in range(2):
            first, second = halves(tri[half * 32 : half * 32 + 16], tri[half * 32 + 16 : half * 32 + 32])
            at = slot * 2 + half
            wide[pl.ds(at, 16, stride=8), :] = first
            wide[pl.ds(128 + at, 16, stride=8), :] = second
    send3[...] = wide[0:256, :].reshape(32, 8, C).astype(BF16)
    recv3[pl.ds(group, 1)] = send3[pl.ds(group, 1)]

    @pl.loop(1, 32)
    def _(step):
        to = (group + step) % 32
        remote(send3.at[to], recv3.at[group], s_3, r_3, plane(to)).start()

    remote(tok_recv.at[pl.ds(0, 3)], x_recv.at[pl.ds(0, 3)], s_x, r_x, mate).wait_recv()
    tot_ref[0:16, :] = jnp.sum(x_recv[...], axis=0)
    count = tot_ref[12:20, :]
    single = jnp.concatenate([tot_ref[4 * k : 4 * k + 8, :] / count for k in range(3)], axis=1).astype(BF16)
    k_send[...] = dot(single, w_col_ref[...])
    r_send[...] = dot(single, w_row_ref[...])
    k_recv[pl.ds(p, 1)] = k_send[...][None]

    @pl.when(diagonal)
    def _():
        r_recv[...] = r_send[...]

    @pl.when(jnp.logical_not(diagonal))
    def _():
        remote(r_send, r_recv, s_r, r_r, flipped).start()

    @pl.loop(1, 16)
    def _(step):
        to = z_hi * 16 + (p + step) % 16
        remote(k_send, k_recv.at[p], s_k, r_k, plane(to)).start()

    remote(send3.at[pl.ds(0, 31)], recv3.at[pl.ds(0, 31)], s_3, r_3, mate).wait_recv()
    wide[0:256, :] = recv3[...].reshape(256, C).astype(F32)
    for half in range(2):
        tri = jnp.concatenate(
            [wide[pl.ds(slot * 2 + half, 32, stride=8), :] for slot in range(4)], axis=0
        )
        centered = tri - jnp.mean(tri, axis=0, keepdims=True)
        variance = jnp.mean(centered * centered, axis=0, keepdims=True)
        tri_norm = (centered * lax.rsqrt(variance + 1e-05)).T.astype(BF16)
        update = dot(tri_norm, tri_out_ref[...])
        for odd in range(2):
            for i in range(4):
                upd_ref[pl.ds((half * 2 + odd) * 64 + i, 16, stride=4), :] = update[
                    odd * 64 + i * 16 : odd * 64 + i * 16 + 16
                ]
    update = pair_ref[...].reshape(256, C).astype(F32) + upd_ref[...] * gate_ref[...]

    remote(tok_recv.at[pl.ds(0, 15), pl.ds(0, 8)], k_recv.at[pl.ds(0, 15)], s_k, r_k, mate).wait_recv()

    @pl.when(jnp.logical_not(diagonal))
    def _():
        remote(r_send, r_recv, s_r, r_r, flipped).wait_recv()

    k_term = k_recv[...][:, 0:4, :].reshape(64, C)
    for i in range(4):
        pair_out_ref[i] = (update[i * 64 : i * 64 + 64] + k_term + r_recv[i : i + 1, :]).astype(BF16)

    to_next.wait_send()
    to_prev.wait_send()
    to_mate.wait_send()
    remote(send1.at[pl.ds(0, 31)], recv1.at[pl.ds(0, 31)], s_1, r_1, mate).wait_send()
    remote(tok_send.at[pl.ds(0, 15)], tok_recv.at[pl.ds(0, 15)], s_t, r_t, mate).wait_send()
    remote(send3.at[pl.ds(0, 31)], recv3.at[pl.ds(0, 31)], s_3, r_3, mate).wait_send()
    remote(x_recv.at[pl.ds(0, 3)], x_recv.at[pl.ds(0, 3)], s_x, r_x, mate).wait_send()
    remote(k_recv.at[pl.ds(0, 15)], k_recv.at[pl.ds(0, 15)], s_k, r_k, mate).wait_send()
    for step in range(1, 4):
        remote(right, rights.at[0], s_2.at[step], r_2.at[0], mate).wait_send()

    @pl.when(jnp.logical_not(own_right))
    def _():
        remote(right, rights.at[0], s_2.at[0], r_2.at[0], mate).wait_send()

    @pl.when(jnp.logical_not(diagonal))
    def _():
        remote(r_send, r_recv, s_r, r_r, flipped).wait_send()


def per_device(
    pair, atoms, atom_token, tri_proj, tri_out, w_qkv, w_attn_out, w_token, w_row, w_col
):
    vmem = pl.BlockSpec(memory_space=pltpu.VMEM)
    sem = pltpu.SemaphoreType.DMA
    return pl.pallas_call(
        kernel,
        out_shape=(
            jax.ShapeDtypeStruct(pair.shape, BF16),
            jax.ShapeDtypeStruct(atoms.shape, BF16),
        ),
        in_specs=[vmem] * 10,
        out_specs=(vmem, vmem),
        scratch_shapes=[
            pltpu.VMEM((512, C), F32),
            pltpu.VMEM((32, 16, C), BF16),
            pltpu.VMEM((32, 16, C), BF16),
            pltpu.VMEM((2, 4, 64, C), BF16),
            pltpu.VMEM((4, 64, C), BF16),
            pltpu.VMEM((4, 4, 64, C), BF16),
            pltpu.VMEM((32, 8, C), BF16),
            pltpu.VMEM((32, 8, C), BF16),
            pltpu.VMEM((256, C), F32),
            pltpu.VMEM((256, C), F32),
            pltpu.VMEM((48, C), BF16),
            pltpu.VMEM((48, C), BF16),
            pltpu.VMEM((16, 16, C), F32),
            pltpu.VMEM((16, 16, C), F32),
            pltpu.VMEM((16, C), F32),
            pltpu.VMEM((4, 16, C), F32),
            pltpu.VMEM((24, C), F32),
            pltpu.VMEM((8, C), F32),
            pltpu.VMEM((16, 8, C), F32),
            pltpu.VMEM((8, C), F32),
            pltpu.VMEM((8, C), F32),
            sem((2,)), sem((2,)),
            sem, sem,
            sem((4,)), sem((4,)),
            sem, sem,
            sem, sem,
            sem, sem,
            sem, sem,
            sem, sem,
            sem, sem,
        ],
        compiler_params=pltpu.CompilerParams(
            collective_id=0, has_side_effects=True, vmem_limit_bytes=32 << 20
        ),
    )(
        pair, atoms, atom_token.reshape(1, 128), tri_proj, tri_out, w_qkv, w_attn_out, w_token,
        w_row, w_col,
    )


def solution(mesh):
    return jax.shard_map(
        per_device,
        mesh=mesh,
        in_specs=(
            P("row", "col", None),
            P("row", None),
            P("row"),
            P(),
            P(),
            P(),
            P(),
            P(),
            P(),
            P(),
        ),
        out_specs=(P("row", "col", None), P("row", None)),
        check_vma=False,
    )
```

time: 1180 us -> 41.8 us (0.04)
  the two profiles are of different devices: /device:TPU:128 before, /device:TPU:4 now
where the time goes in v1:
time: 41.8 us; the launch traced here: 41.3 us
  Pallas kernels  31.2 us (75%)
  local copies, waits for them, and re-layouts  9.49 us (23%)
  between operations  0.66 us (2%)
    pallas_call x1, Pallas kernels, per_device(): pl.pallas_call(kernel, out_shape=(jax.ShapeDtypeStruct(pair.shape, BF16),...  31.2 us
    unnamed x22, local copies, waits for them, and re-layouts  9.49 us

profile of v1, /device:TPU:4, one launch (start us, length us, event | category | flops | bytes accessed | tf_op | source)
XLA Modules:
  0.0 41.3 jit_solution(15311633523184949074)
XLA Ops:
  0.6 0.0 copy-start.9
  0.6 0.6 %copy-done.9 = s32[128]{0:T(128)S(1)} copy-done((s32[128]{0:T(128)S(1)}, s32[128]{0:T(128)}, u32[]{:S(2)}) %copy-start.9) | copy-done | bytes 536
  1.3 0.0 copy-start
  1.3 0.9 %copy-done = bf16[128,640]{1,0:T(8,128)(2,1)S(1)} copy-done((bf16[128,640]{1,0:T(8,128)(2,1)S(1)}, bf16[128,640]{1,0:T(8,128)(2,1)}, u32[]{:S(2)}) %copy-start) | copy-done | bytes 163864
  2.2 0.0 copy-start.1
  2.2 0.9 %copy-done.1 = bf16[128,384]{1,0:T(8,128)(2,1)S(1)} copy-done((bf16[128,384]{1,0:T(8,128)(2,1)S(1)}, bf16[128,384]{1,0:T(8,128)(2,1)}, u32[]{:S(2)}) %copy-start.1) | copy-done | bytes 98328
  3.1 0.0 copy-start.2
  3.1 0.9 %copy-done.2 = bf16[128,384]{1,0:T(8,128)(2,1)S(1)} copy-done((bf16[128,384]{1,0:T(8,128)(2,1)S(1)}, bf16[128,384]{1,0:T(8,128)(2,1)}, u32[]{:S(2)}) %copy-start.2) | copy-done | bytes 98328
  4.0 0.0 copy-start.3
  4.0 0.9 %copy-done.3 = bf16[384,128]{1,0:T(8,128)(2,1)S(1)} copy-done((bf16[384,128]{1,0:T(8,128)(2,1)S(1)}, bf16[384,128]{1,0:T(8,128)(2,1)}, u32[]{:S(2)}) %copy-start.3) | copy-done | bytes 98328
  4.9 0.0 copy-start.4
  4.9 0.9 %copy-done.4 = bf16[384,128]{1,0:T(8,128)(2,1)S(1)} copy-done((bf16[384,128]{1,0:T(8,128)(2,1)S(1)}, bf16[384,128]{1,0:T(8,128)(2,1)}, u32[]{:S(2)}) %copy-start.4) | copy-done | bytes 98328
  5.8 0.0 copy-start.5
  5.8 0.8 %copy-done.5 = bf16[4,64,128]{2,1,0:T(8,128)(2,1)S(1)} copy-done((bf16[4,64,128]{2,1,0:T(8,128)(2,1)S(1)}, bf16[4,64,128]{2,1,0:T(8,128)(2,1)}, u32[]{:S(2)}) %copy-start.5) | copy-done | bytes 65560
  6.6 0.0 copy-start.6
  6.6 0.8 %copy-done.6 = bf16[128,128]{1,0:T(8,128)(2,1)S(1)} copy-done((bf16[128,128]{1,0:T(8,128)(2,1)S(1)}, bf16[128,128]{1,0:T(8,128)(2,1)}, u32[]{:S(2)}) %copy-start.6) | copy-done | bytes 32792
  7.4 0.0 copy-start.7
  7.4 0.8 %copy-done.7 = bf16[128,128]{1,0:T(8,128)(2,1)S(1)} copy-done((bf16[128,128]{1,0:T(8,128)(2,1)S(1)}, bf16[128,128]{1,0:T(8,128)(2,1)}, u32[]{:S(2)}) %copy-start.7) | copy-done | bytes 32792
  8.1 0.0 copy-start.8
  8.1 0.8 %copy-done.8 = bf16[128,128]{1,0:T(8,128)(2,1)S(1)} copy-done((bf16[128,128]{1,0:T(8,128)(2,1)S(1)}, bf16[128,128]{1,0:T(8,128)(2,1)}, u32[]{:S(2)}) %copy-start.8) | copy-done | bytes 32792
  8.9 31.2 %shard_map.113 = (bf16[4,64,128]{2,1,0:T(8,128)(2,1)S(1)}, bf16[128,128]{1,0:T(8,128)(2,1)S(1)}) custom-call(bf16[4,64,128]{2,1,0:T(8,128)(2,1)S(1)} %copy-done.5, bf16[128,128]{1,0:T(8,128)(2,1)S(1)} %copy-done.6, s32[1,128]{1,0:T(1,128)S(1)} %bitcast.1, bf16[128,640]{1,0:T(8,128)(2,1)S(1)} %copy-done, bf16[128,128]{1,0:T(8,128)(2,1)S(1)} %copy-done.7, ...), custom_call_target="tpu_custom_call" | custom-call | tf_op jit(solution)/shard_map/pallas_call | solution.py:326
  40.1 0.6 %copy.14 = bf16[4,64,128]{2,1,0:T(8,128)(2,1)} copy(bf16[4,64,128]{2,1,0:T(8,128)(2,1)S(1)} %get-tuple-element.4) | data formatting | bytes 131072
  40.7 0.6 %copy.15 = bf16[128,128]{1,0:T(8,128)(2,1)} copy(bf16[128,128]{1,0:T(8,128)(2,1)S(1)} %get-tuple-element.5) | data formatting | bytes 65536
Async XLA Ops:
  0.6 0.7 %copy-start.9 = (s32[128]{0:T(128)S(1)}, s32[128]{0:T(128)}, u32[]{:S(2)}) copy-start(s32[128]{0:T(128)} %param.12) | copy-start | bytes 1540
  1.3 0.9 %copy-start = (bf16[128,640]{1,0:T(8,128)(2,1)S(1)}, bf16[128,640]{1,0:T(8,128)(2,1)}, u32[]{:S(2)}) copy-start(bf16[128,640]{1,0:T(8,128)(2,1)} %tri_proj_ref.1) | copy-start | bytes 491524
  2.2 0.9 %copy-start.1 = (bf16[128,384]{1,0:T(8,128)(2,1)S(1)}, bf16[128,384]{1,0:T(8,128)(2,1)}, u32[]{:S(2)}) copy-start(bf16[128,384]{1,0:T(8,128)(2,1)} %w_qkv_ref.1) | copy-start | bytes 294916
  3.1 0.9 %copy-start.2 = (bf16[128,384]{1,0:T(8,128)(2,1)S(1)}, bf16[128,384]{1,0:T(8,128)(2,1)}, u32[]{:S(2)}) copy-start(bf16[128,384]{1,0:T(8,128)(2,1)} %w_token_ref.1) | copy-start | bytes 294916
  4.0 0.9 %copy-start.3 = (bf16[384,128]{1,0:T(8,128)(2,1)S(1)}, bf16[384,128]{1,0:T(8,128)(2,1)}, u32[]{:S(2)}) copy-start(bf16[384,128]{1,0:T(8,128)(2,1)} %w_row_ref.1) | copy-start | bytes 294916
  4.9 0.9 %copy-start.4 = (bf16[384,128]{1,0:T(8,128)(2,1)S(1)}, bf16[384,128]{1,0:T(8,128)(2,1)}, u32[]{:S(2)}) copy-start(bf16[384,128]{1,0:T(8,128)(2,1)} %w_col_ref.1) | copy-start | bytes 294916
  5.8 0.8 %copy-start.5 = (bf16[4,64,128]{2,1,0:T(8,128)(2,1)S(1)}, bf16[4,64,128]{2,1,0:T(8,128)(2,1)}, u32[]{:S(2)}) copy-start(bf16[4,64,128]{2,1,0:T(8,128)(2,1)} %pair_ref.1) | copy-start | bytes 196612
  6.6 0.8 %copy-start.6 = (bf16[128,128]{1,0:T(8,128)(2,1)S(1)}, bf16[128,128]{1,0:T(8,128)(2,1)}, u32[]{:S(2)}) copy-start(bf16[128,128]{1,0:T(8,128)(2,1)} %atoms_ref.1) | copy-start | bytes 98308
  7.4 0.8 %copy-start.7 = (bf16[128,128]{1,0:T(8,128)(2,1)S(1)}, bf16[128,128]{1,0:T(8,128)(2,1)}, u32[]{:S(2)}) copy-start(bf16[128,128]{1,0:T(8,128)(2,1)} %tri_out_ref.1) | copy-start | bytes 98308
  8.1 0.8 %copy-start.8 = (bf16[128,128]{1,0:T(8,128)(2,1)S(1)}, bf16[128,128]{1,0:T(8,128)(2,1)}, u32[]{:S(2)}) copy-start(bf16[128,128]{1,0:T(8,128)(2,1)} %w_attn_ref.1) | copy-start | bytes 98308

commit v2 on v1

--- a/solution.py
+++ b/solution.py
@@ -41,11 +41,14 @@
 
 
 def kernel(
+    pair_in, atoms_in, token_in, tri_proj_in, tri_out_in, w_qkv_in, w_attn_in, w_token_in, w_row_in,
+    w_col_in, pair_out_ref, atom_out_ref,
     pair_ref, atoms_ref, token_ref, tri_proj_ref, tri_out_ref, w_qkv_ref, w_attn_ref, w_token_ref,
-    w_row_ref, w_col_ref, pair_out_ref, atom_out_ref,
+    w_row_ref, w_col_ref,
     wide, send1, recv1, left, right, rights, send3, recv3, gate_ref, upd_ref,
     before, after, tok_send, tok_recv, x_send, x_recv, tot_ref, k_send, k_recv, r_send, r_recv,
     s_halo, r_halo, s_1, r_1, s_2, r_2, s_l, r_l, s_3, r_3, s_t, r_t, s_x, r_x, s_k, r_k, s_r, r_r,
+    s_in,
 ):
     row, col = lax.axis_index("row"), lax.axis_index("col")
     x, p = row // 16, row % 16
@@ -89,6 +92,26 @@
             src_ref=src, dst_ref=dst, send_sem=send_sem, recv_sem=recv_sem, device_id=to, device_id_type=MESH
         )
 
+    arguments = [
+        pltpu.make_async_copy(source, target, s_in.at[k])
+        for k, (source, target) in enumerate(
+            (
+                (pair_in, pair_ref),
+                (tri_proj_in, tri_proj_ref),
+                (atoms_in, atoms_ref),
+                (w_qkv_in, w_qkv_ref),
+                (w_attn_in, w_attn_ref),
+                (w_token_in, w_token_ref),
+                (token_in, token_ref),
+                (tri_out_in, tri_out_ref),
+                (w_row_in, w_row_ref),
+                (w_col_in, w_col_ref),
+            )
+        )
+    ]
+    for k in range(3):
+        arguments[k].start()
+
     barrier = pltpu.get_barrier_semaphore()
 
     def hello(to):
@@ -112,6 +135,11 @@
     def _():
         hello(flipped)
 
+    for k in range(3, 10):
+        arguments[k].start()
+
+    arguments[0].wait()
+    arguments[1].wait()
     pair_norm = normed(pair_ref[...].reshape(256, C).astype(F32)).astype(BF16)
     for side in range(2):
         at = 2 * side * C
@@ -128,6 +156,7 @@
 
     pl.semaphore_wait(barrier, 2 + 31 + 6 + 1 + jnp.where(diagonal, 0, 1))
 
+    arguments[2].wait()
     to_next = remote(atoms_ref.at[pl.ds(80, 48)], before, s_halo.at[0], r_halo.at[0], next_row())
     to_prev = remote(atoms_ref.at[pl.ds(0, 48)], after, s_halo.at[1], r_halo.at[1], prev_row())
     to_next.start()
@@ -140,6 +169,8 @@
 
     gate_ref[...] = sigmoid(dot(pair_norm, tri_proj_ref[:, 4 * C :]))
 
+    for k in range(3, 7):
+        arguments[k].wait()
     to_next.wait_recv()
     to_prev.wait_recv()
     atoms = atoms_ref[...].astype(F32)
@@ -250,6 +281,9 @@
         to = (group + step) % 32
         remote(send3.at[to], recv3.at[group], s_3, r_3, plane(to)).start()
 
+    for k in range(7, 10):
+        arguments[k].wait()
+
     remote(tok_recv.at[pl.ds(0, 3)], x_recv.at[pl.ds(0, 3)], s_x, r_x, mate).wait_recv()
     tot_ref[0:16, :] = jnp.sum(x_recv[...], axis=0)
     count = tot_ref[12:20, :]
@@ -329,9 +363,19 @@
             jax.ShapeDtypeStruct(pair.shape, BF16),
             jax.ShapeDtypeStruct(atoms.shape, BF16),
         ),
-        in_specs=[vmem] * 10,
+        in_specs=[pl.BlockSpec(memory_space=pltpu.HBM)] * 10,
         out_specs=(vmem, vmem),
         scratch_shapes=[
+            pltpu.VMEM(pair.shape, BF16),
+            pltpu.VMEM(atoms.shape, BF16),
+            pltpu.VMEM((1, 128), jnp.int32),
+            pltpu.VMEM(tri_proj.shape, BF16),
+            pltpu.VMEM(tri_out.shape, BF16),
+            pltpu.VMEM(w_qkv.shape, BF16),
+            pltpu.VMEM(w_attn_out.shape, BF16),
+            pltpu.VMEM(w_token.shape, BF16),
+            pltpu.VMEM(w_row.shape, BF16),
+            pltpu.VMEM(w_col.shape, BF16),
             pltpu.VMEM((512, C), F32),
             pltpu.VMEM((32, 16, C), BF16),
             pltpu.VMEM((32, 16, C), BF16),
@@ -362,9 +406,10 @@
             sem, sem,
             sem, sem,
             sem, sem,
+            sem((10,)),
         ],
         compiler_params=pltpu.CompilerParams(
-            collective_id=0, has_side_effects=True, vmem_limit_bytes=32 << 20
+            collective_id=0, has_side_effects=True, vmem_limit_bytes=60 << 20
         ),
     )(
         pair, atoms, atom_token.reshape(1, 128), tri_proj, tri_out, w_qkv, w_attn_out, w_token,

time: 41.8 us -> 35.3 us (0.84)
  local copies, waits for them, and re-layouts: 9.49 us -> 2.1 us
  Pallas kernels: 31.2 us -> 32.4 us
    unnamed x22 -> x4, local copies, waits for them, and re-layouts: 9.49 us -> 2.1 us
    pallas_call x1, Pallas kernels: 31.2 us -> 32.4 us  [per_device(): pl.pallas_call(kernel, out_shape=(jax.ShapeDtypeStruct(pair.shape, BF16),...]
where the time goes in v2:
time: 35.3 us; the launch traced here: 35.2 us
  Pallas kernels  32.4 us (92%)
  local copies, waits for them, and re-layouts  2.1 us (6%)
  between operations  0.65 us (2%)
    pallas_call x1, Pallas kernels, per_device(): pl.pallas_call(kernel, out_shape=(jax.ShapeDtypeStruct(pair.shape, BF16),...  32.4 us
    unnamed x4, local copies, waits for them, and re-layouts  2.1 us

profile of v2, /device:TPU:4, one launch (start us, length us, event | category | flops | bytes accessed | tf_op | source)
XLA Modules:
  0.0 35.2 jit_solution(1984343258496755951)
XLA Ops:
  0.6 32.4 %shard_map.113 = (bf16[4,64,128]{2,1,0:T(8,128)(2,1)}, bf16[128,128]{1,0:T(8,128)(2,1)}) custom-call(bf16[4,64,128]{2,1,0:T(8,128)(2,1)} %pair_in.1, bf16[128,128]{1,0:T(8,128)(2,1)} %atoms_in.1, s32[1,128]{1,0:T(1,128)} %bitcast.1, bf16[128,640]{1,0:T(8,128)(2,1)} %tri_proj_in.1, bf16[128,128]{1,0:T(8,128)(2,1)} %tri_out_in.1, bf16[128,384]{1,0:T(8,128)(2,1)} %w_qkv_in.1, ...), custom_call_target="tpu_custom_call" | custom-call | tf_op jit(solution)/shard_map/pallas_call | solution.py:360
  33.1 0.0 copy-start
  33.1 1.5 %copy.14 = bf16[4,64,128]{2,1,0:T(8,128)(2,1)} copy(bf16[4,64,128]{2,1,0:T(8,128)(2,1)} %get-tuple-element.4) | data formatting | bytes 131072
  34.6 0.0 copy-done
  34.6 0.6 %copy.15 = bf16[128,128]{1,0:T(8,128)(2,1)} copy(bf16[128,128]{1,0:T(8,128)(2,1)S(1)} %copy-done) | data formatting | bytes 65536
Async XLA Ops:
  33.1 1.5 %copy-start = (bf16[128,128]{1,0:T(8,128)(2,1)S(1)}, bf16[128,128]{1,0:T(8,128)(2,1)}, u32[]{:S(2)}) copy-start(bf16[128,128]{1,0:T(8,128)(2,1)} %get-tuple-element.5) | copy-start | bytes 98308

commit v3 on v2

--- a/solution.py
+++ b/solution.py
@@ -352,17 +352,27 @@
         remote(r_send, r_recv, s_r, r_r, flipped).wait_send()
 
 
+def store(pair_in, atoms_in, pair_to, atoms_to, done):
+    first = pltpu.make_async_copy(pair_in, pair_to, done.at[0])
+    second = pltpu.make_async_copy(atoms_in, atoms_to, done.at[1])
+    first.start()
+    second.start()
+    first.wait()
+    second.wait()
+
+
 def per_device(
     pair, atoms, atom_token, tri_proj, tri_out, w_qkv, w_attn_out, w_token, w_row, w_col
 ):
     vmem = pl.BlockSpec(memory_space=pltpu.VMEM)
     sem = pltpu.SemaphoreType.DMA
-    return pl.pallas_call(
+    arguments = (
+        pair, atoms, atom_token.reshape(1, 128), tri_proj, tri_out, w_qkv, w_attn_out, w_token,
+        w_row, w_col,
+    )
+    results = pl.pallas_call(
         kernel,
-        out_shape=(
-            jax.ShapeDtypeStruct(pair.shape, BF16),
-            jax.ShapeDtypeStruct(atoms.shape, BF16),
-        ),
+        out_shape=(pltpu.VMEM(pair.shape, BF16), pltpu.VMEM(atoms.shape, BF16)),
         in_specs=[pl.BlockSpec(memory_space=pltpu.HBM)] * 10,
         out_specs=(vmem, vmem),
         scratch_shapes=[
@@ -409,12 +419,20 @@
             sem((10,)),
         ],
         compiler_params=pltpu.CompilerParams(
-            collective_id=0, has_side_effects=True, vmem_limit_bytes=60 << 20
+            collective_id=0, has_side_effects=True, vmem_limit_bytes=32 << 20
         ),
-    )(
-        pair, atoms, atom_token.reshape(1, 128), tri_proj, tri_out, w_qkv, w_attn_out, w_token,
-        w_row, w_col,
-    )
+    )(*(pltpu.with_memory_space_constraint(value, pltpu.HBM) for value in arguments))
+    hbm = pl.BlockSpec(memory_space=pltpu.HBM)
+    return pl.pallas_call(
+        store,
+        out_shape=(
+            jax.ShapeDtypeStruct(pair.shape, BF16),
+            jax.ShapeDtypeStruct(atoms.shape, BF16),
+        ),
+        in_specs=[vmem, vmem],
+        out_specs=(hbm, hbm),
+        scratch_shapes=[sem((2,))],
+    )(*(pltpu.with_memory_space_constraint(value, pltpu.VMEM) for value in results))
 
 
 def solution(mesh):

time: 35.3 us -> 33.2 us (0.941)
  local copies, waits for them, and re-layouts: 2.1 us -> 0 us
    unnamed x4 -> x0, local copies, waits for them, and re-layouts: 2.1 us -> none
    pallas_call x1 -> x2, Pallas kernels: 32.4 us -> 32.5 us  [the longest x1 31.8 us: per_device(): pl.pallas_call(kernel, out_shape=(pltpu.VMEM(pair.shape, BF16), pltpu.VME...]
where the time goes in v3:
time: 33.2 us; the launch traced here: 33.1 us
  Pallas kernels  32.5 us (98%)
  between operations  0.64 us (2%)
    pallas_call x1, Pallas kernels, per_device(): pl.pallas_call(kernel, out_shape=(pltpu.VMEM(pair.shape, BF16), pltpu.VME...  31.8 us

profile of v3, /device:TPU:4, one launch (start us, length us, event | category | flops | bytes accessed | tf_op | source)
XLA Modules:
  0.0 33.1 jit_solution(2606027168646201378)
XLA Ops:
  0.6 31.8 %shard_map.113 = (bf16[4,64,128]{2,1,0:T(8,128)(2,1)S(1)}, bf16[128,128]{1,0:T(8,128)(2,1)S(1)}) custom-call(bf16[4,64,128]{2,1,0:T(8,128)(2,1)} %pair_in.1, bf16[128,128]{1,0:T(8,128)(2,1)} %atoms_in.1, s32[1,128]{1,0:T(1,128)} %bitcast.1, bf16[128,640]{1,0:T(8,128)(2,1)} %tri_proj_in.1, bf16[128,128]{1,0:T(8,128)(2,1)} %tri_out_in.1, ...), custom_call_target="tpu_custom_call" | custom-call | tf_op jit(solution)/shard_map/pallas_call | solution.py:373
  32.5 0.7 %shard_map.114 = (bf16[4,64,128]{2,1,0:T(8,128)(2,1)}, bf16[128,128]{1,0:T(8,128)(2,1)}) custom-call(bf16[4,64,128]{2,1,0:T(8,128)(2,1)S(1)} %get-tuple-element.4.pair_in, bf16[128,128]{1,0:T(8,128)(2,1)S(1)} %get-tuple-element.5.atoms_in), custom_call_target="tpu_custom_call" | custom-call | tf_op jit(solution)/shard_map/pallas_call | solution.py:426

commit v4 on v3

v4 whole, which is shorter than its diff:
```python
import functools

import jax
import jax.numpy as jnp
from jax import lax
from jax.experimental import pallas as pl
from jax.experimental.pallas import tpu as pltpu
from jax.sharding import PartitionSpec as P

MESH = pl.DeviceIdType.MESH
F32 = jnp.float32
BF16 = jnp.bfloat16
HEADS = 4
C = 128


def normed(values):
    mean = jnp.mean(values, axis=-1, keepdims=True)
    centered = values - mean
    variance = jnp.mean(centered * centered, axis=-1, keepdims=True)
    return centered * lax.rsqrt(variance + 1e-05)


def sigmoid(values):
    return 0.5 * jnp.tanh(0.5 * values) + 0.5


def dot(a, b):
    return jnp.dot(a, b, preferred_element_type=F32)


def dot_nt(a, b):
    return lax.dot_general(a, b, (((1,), (1,)), ((), ())), preferred_element_type=F32)


def halves(low, high):
    lane = lax.broadcasted_iota(jnp.int32, low.shape, 1)
    even = jnp.where(lane < 64, low, pltpu.roll(high, 64, 1))
    odd = jnp.where(lane < 64, pltpu.roll(low, 64, 1), high)
    return even, odd


def kernel(
    pair_in, atoms_in, token_in, tri_proj_in, tri_out_in, w_qkv_in, w_attn_in, w_token_in, w_row_in,
    w_col_in, pair_out_ref, atom_out_ref,
    pair_ref, atoms_ref, token_ref, tri_proj_ref, tri_out_ref, w_qkv_ref, w_attn_ref, w_token_ref,
    w_row_ref, w_col_ref,
    wide, send1, recv1, left, right, rights, send3, recv3, gate_ref, upd_ref,
    before, after, tok_send, tok_recv, k_send, k_recv, r_send, r_recv,
    s_halo, r_halo, s_1, r_1, s_2, r_2, s_l, r_l, s_3, r_3, s_t, r_t, s_k, r_k, s_r, r_r,
    s_in, plane_in,
):
    row, col = lax.axis_index("row"), lax.axis_index("col")
    x, p = row // 16, row % 16
    y, z_lo = p // 4, p % 4
    z_hi, core = col // 2, col % 2
    z = z_hi * 4 + z_lo
    group = z_hi * 16 + p
    parity = x % 2

    ys = [(y + step) % 4 for step in range(4)]

    def place_of(x_to, y_to, z_to):
        return (x_to * 16 + y_to * 4 + z_to % 4, 2 * (z_to // 4) + core)

    def plane(act):
        @pl.loop(0, 7)
        def _(k):
            z_to = (z + 4 + ((k + 1) // 2) * (1 - 2 * (k % 2))) % 8
            for step in (2, 1, 3, 0):
                act((z_to // 4) * 16 + ys[step] * 4 + z_to % 4, place_of(x, ys[step], z_to))

        for step in (2, 1, 3):
            act(z_hi * 16 + ys[step] * 4 + z_lo, place_of(x, ys[step], z))

    def other_x(act, z_steps):
        @pl.loop(0, 3)
        def _(k):
            x_to = (x + 2 + ((k + 1) // 2) * (1 - 2 * (k % 2))) % 4
            for z_step in z_steps:
                z_to = (z + z_step) % 8
                for step in (2, 1, 3, 0):
                    act(x_to, ys[step] * 4 + z_to % 4, place_of(x_to, ys[step], z_to))

    def same_x(act, z_steps):
        for z_step in z_steps:
            z_to = (z + z_step) % 8
            for step in (2, 1, 3, 0):
                if step or z_step:
                    act(x, ys[step] * 4 + z_to % 4, place_of(x, ys[step], z_to))

    def next_row():
        carry_y = (z_lo + 1) // 4
        carry_x = (y + carry_y) // 4
        z_to = (z + 1) % 8
        row_to = ((x + carry_x) % 4) * 16 + ((y + carry_y) % 4) * 4 + z_to % 4
        return (row_to, 2 * (z_to // 4) + core)

    def prev_row():
        carry_y = (4 - z_lo) // 4
        carry_x = (3 - y + carry_y) // 4
        z_to = (z + 7) % 8
        row_to = ((x + 4 - carry_x) % 4) * 16 + ((y + 4 - carry_y) % 4) * 4 + z_to % 4
        return (row_to, 2 * (z_to // 4) + core)

    def along_x(step, core_to):
        return (((x + step) % 4) * 16 + p, 2 * z_hi + core_to)

    mate = (row, 2 * z_hi + 1 - core)
    own_right = parity == core

    def remote(src, dst, send_sem, recv_sem, to):
        return pltpu.make_async_remote_copy(
            src_ref=src, dst_ref=dst, send_sem=send_sem, recv_sem=recv_sem, device_id=to, device_id_type=MESH
        )

    arguments = [
        pltpu.make_async_copy(source, target, s_in.at[k])
        for k, (source, target) in enumerate(
            (
                (pair_in, pair_ref),
                (tri_proj_in, tri_proj_ref),
                (atoms_in, atoms_ref),
                (w_qkv_in, w_qkv_ref),
                (w_attn_in, w_attn_ref),
                (w_token_in, w_token_ref),
                (token_in, token_ref),
                (tri_out_in, tri_out_ref),
                (w_row_in, w_row_ref),
                (w_col_in, w_col_ref),
            )
        )
    ]
    for k in range(3):
        arguments[k].start()

    barrier = pltpu.get_barrier_semaphore()

    def hello(to):
        pl.semaphore_signal(barrier, inc=1, device_id=to, device_id_type=MESH)

    plane(lambda group_to, to: hello(to))
    for step in (2, 1, 3):
        hello(along_x(step, core))
        hello(along_x(step, 1 - core))
    hello(next_row())
    hello(prev_row())
    hello(mate)

    for k in range(3, 10):
        arguments[k].start()

    arguments[0].wait()
    arguments[1].wait()
    pair_norm = normed(pair_ref[...].reshape(256, C).astype(F32)).astype(BF16)
    for side in range(2):
        at = 2 * side * C
        gated = sigmoid(dot(pair_norm, tri_proj_ref[:, at : at + C])) * dot(
            pair_norm, tri_proj_ref[:, at + C : at + 2 * C]
        )
        for half in range(2):
            flat = gated[half * 128 : half * 128 + 128].T
            for slot in range(4):
                wide[pl.ds(side * 8 + slot * 2 + half, 32, stride=16), :] = flat[slot * 32 : slot * 32 + 32]
    send1[...] = wide[...].reshape(32, 16, C).astype(BF16)
    recv1[pl.ds(group, 1)] = send1[pl.ds(group, 1)]
    gate_ref[...] = sigmoid(dot(pair_norm, tri_proj_ref[:, 4 * C :]))

    pl.semaphore_wait(barrier, 31 + 6 + 2 + 1)
    for step in (2, 1, 3):
        pl.semaphore_signal(plane_in, inc=1, device_id=along_x(step, core), device_id_type=MESH)

    arguments[2].wait()
    to_next = remote(atoms_ref.at[pl.ds(80, 48)], before, s_halo.at[0], r_halo.at[0], next_row())
    to_prev = remote(atoms_ref.at[pl.ds(0, 48)], after, s_halo.at[1], r_halo.at[1], prev_row())
    to_next.start()
    to_prev.start()

    plane(lambda group_to, to: remote(send1.at[group_to], recv1.at[group], s_1, r_1, to).start())

    for k in range(3, 10):
        arguments[k].wait()
    atoms = atoms_ref[...].astype(F32)
    own = dot(normed(atoms).astype(BF16), w_qkv_ref[...]).astype(BF16)
    line = lax.broadcasted_iota(jnp.int32, (128, 128), 0)
    lane = lax.broadcasted_iota(jnp.int32, (128, 128), 1)
    token_id = 64 * (2 * ((line // 4) % 2) + core) + 4 * (line // 8) + line % 4
    picked = jnp.where(token_id == token_ref[...], 1.0, 0.0).astype(BF16)
    to_next.wait_recv()
    to_prev.wait_recv()
    edge = jnp.concatenate([before[...], after[...]], axis=0).astype(F32)
    edge = dot(normed(edge).astype(BF16), w_qkv_ref[:, C:]).astype(BF16)
    keys = jnp.concatenate([edge[0:48, :C], own[:, C : 2 * C], edge[48:96, :C]], axis=0)
    values = jnp.concatenate([edge[0:48, C:], own[:, 2 * C :], edge[48:96, C:]], axis=0)
    head_of = lax.broadcasted_iota(jnp.int32, (32, C), 1) // 32
    attended = []
    for window in range(4):
        at = 32 * window
        query = own[at : at + 32, :C]
        query = jnp.concatenate(
            [jnp.where(head_of == h, query, jnp.zeros_like(query)) for h in range(HEADS)], axis=0
        )
        scores = dot_nt(query, keys[at : at + 128]) * (32.0**-0.5)
        position = row * 128 + at - 48 + lax.broadcasted_iota(jnp.int32, (128, 128), 1)
        scores = jnp.where((position >= 0) & (position < 8192), scores, -1e30)
        probs = jnp.exp(scores - jnp.max(scores, axis=-1, keepdims=True))
        probs = (probs / jnp.sum(probs, axis=-1, keepdims=True)).astype(BF16)
        mixed = dot(probs, values[at : at + 128])
        result = mixed[0:32]
        for h in range(1, HEADS):
            result = jnp.where(head_of == h, mixed[32 * h : 32 * h + 32], result)
        attended.append(result)
    attended = jnp.concatenate(attended, axis=0).astype(BF16)
    remote(send1.at[pl.ds(0, 31)], recv1.at[pl.ds(0, 31)], s_1, r_1, mate).wait_recv()
    wide[...] = recv1[...].reshape(512, C).astype(F32)
    place = (x // 2) * 2 + core

    def assemble(side, slot):
        for half in range(2):
            at = side * 8 + slot * 2 + half
            even, odd = halves(
                wide[pl.ds(at, 16, stride=16), :], wide[pl.ds(256 + at, 16, stride=16), :]
            )
            both = jnp.concatenate([even, odd], axis=0).astype(BF16)
            if side:
                right[slot, half * 32 : half * 32 + 32, :] = both
            else:
                left[core, slot, half * 32 : half * 32 + 32, :] = both

    def pass_right(part, step):
        return remote(
            right.at[pl.ds(2 * part, 2)], rights.at[place, pl.ds(2 * part, 2)],
            s_2.at[2 * step + part], r_2.at[2 * place + part], along_x(step, parity),
        )

    for part in range(2):
        assemble(1, 2 * part)
        assemble(1, 2 * part + 1)
        for step in (2, 1, 3):
            pass_right(part, step).start()

        @pl.when(jnp.logical_not(own_right))
        def _():
            pass_right(part, 0).start()

    atom_out = (atoms + dot(attended, w_attn_ref[...])).astype(BF16)
    atom_out_ref[...] = atom_out
    hidden = jnp.maximum(dot(atom_out, w_token_ref[...]), 0.0).astype(BF16)
    summed = dot(picked, hidden).astype(BF16)
    count = jnp.broadcast_to(jnp.sum(picked.astype(F32), axis=1, keepdims=True), (128, C))
    count = jnp.where(lane < 64, pltpu.roll(count.reshape(16, 8, C), 4, 1).reshape(128, C), count)
    k_part = dot(summed, w_col_ref[...])
    r_part = dot(summed, w_row_ref[...])
    r_swap = pltpu.roll(r_part.reshape(16, 8, C), 4, 1).reshape(128, C)
    for high, part in ((0, r_part), (1, r_swap)):
        part = jnp.where(line % 8 < 4, part, count)
        tok_send[high] = jnp.concatenate(
            [k_part.reshape(16, 8, C), part.reshape(16, 8, C)], axis=1
        ).astype(BF16)
    tok_recv[pl.ds(row, 1)] = tok_send[pl.ds(x // 2, 1), pl.ds(p, 1)].reshape(1, 16, C)

    pl.semaphore_wait(plane_in, 3)

    def give(x_to, piece, to):
        remote(tok_send.at[x_to // 2, piece], tok_recv.at[row], s_t, r_t, to).start()

    other_x(give, (2, 7, 1, 0))
    same_x(give, (2, 7, 1, 0))

    @pl.when(own_right)
    def _():
        rights[pl.ds(place, 1)] = right[...][None]

    for slot in range(4):
        assemble(0, slot)
    to_mate = remote(left.at[core], left.at[core], s_l, r_l, mate)
    to_mate.start()

    remote(left.at[1 - core], left.at[1 - core], s_l, r_l, mate).wait_recv()
    for slot in range(4):
        if slot % 2 == 0:
            for source in range(4):

                @pl.when(jnp.logical_not(own_right & (place == source)))
                def _():
                    remote(
                        right.at[pl.ds(slot, 2)], rights.at[source, pl.ds(slot, 2)],
                        s_2.at[0], r_2.at[2 * source + slot // 2], mate,
                    ).wait_recv()

        tri = None
        for k in range(2):
            other = jnp.concatenate([rights[k, slot], rights[2 + k, slot]], axis=0)
            term = dot_nt(left[k, slot], other)
            tri = term if tri is None else tri + term
        for half in range(2):
            first, second = halves(tri[half * 32 : half * 32 + 16], tri[half * 32 + 16 : half * 32 + 32])
            at = slot * 2 + half
            wide[pl.ds(at, 16, stride=8), :] = first
            wide[pl.ds(128 + at, 16, stride=8), :] = second
    send3[...] = wide[0:256, :].reshape(32, 8, C).astype(BF16)
    recv3[pl.ds(group, 1)] = send3[pl.ds(group, 1)]

    plane(lambda group_to, to: remote(send3.at[group_to], recv3.at[group], s_3, r_3, to).start())

    remote(tok_recv.at[pl.ds(0, 63)], tok_recv.at[pl.ds(0, 63)], s_t, r_t, mate).wait_recv()
    total = jnp.sum(tok_recv[...].astype(F32), axis=0)
    count = total[8:16]
    swap = pltpu.roll(count, 64, 1)
    lane, line = lane[0:8], line[0:8]
    low = pltpu.roll(jnp.where(lane < 64, count, swap), 4, 0)
    high = jnp.where(lane < 64, swap, count)
    k_send[...] = total[0:8] / jnp.where(line < 4, low, high)
    k_recv[pl.ds(p, 1)] = k_send[...][None]
    same_x(lambda x_to, piece, to: remote(k_send, k_recv.at[p], s_k, r_k, to).start(), (2, 7, 1, 0))
    count = jnp.where(x // 2 == 0, low, pltpu.roll(high, 4, 0))
    r_send[...] = total[8:16] / jnp.where(line < 4, count, 1.0)

    @pl.when(own_right)
    def _():
        r_recv[...] = r_send[...]
        remote(r_send, r_recv, s_r, r_r, mate).start()

    remote(send3.at[pl.ds(0, 31)], recv3.at[pl.ds(0, 31)], s_3, r_3, mate).wait_recv()
    wide[0:256, :] = recv3[...].reshape(256, C).astype(F32)
    for half in range(2):
        tri = jnp.concatenate(
            [wide[pl.ds(slot * 2 + half, 32, stride=8), :] for slot in range(4)], axis=0
        )
        centered = tri - jnp.mean(tri, axis=0, keepdims=True)
        variance = jnp.mean(centered * centered, axis=0, keepdims=True)
        tri_norm = (centered * lax.rsqrt(variance + 1e-05)).T.astype(BF16)
        update = dot(tri_norm, tri_out_ref[...])
        for odd in range(2):
            for i in range(4):
                upd_ref[pl.ds((half * 2 + odd) * 64 + i, 16, stride=4), :] = update[
                    odd * 64 + i * 16 : odd * 64 + i * 16 + 16
                ]
    update = pair_ref[...].reshape(256, C).astype(F32) + upd_ref[...] * gate_ref[...]

    remote(k_recv.at[pl.ds(0, 15)], k_recv.at[pl.ds(0, 15)], s_k, r_k, mate).wait_recv()

    @pl.when(jnp.logical_not(own_right))
    def _():
        remote(r_send, r_recv, s_r, r_r, mate).wait_recv()

    k_term = k_recv[...]
    k_term = jnp.where(z_hi == 0, k_term[:, 0:4], k_term[:, 4:8]).reshape(64, C)
    r_term = r_recv[...]
    for i in range(4):
        pair_out_ref[i] = (update[i * 64 : i * 64 + 64] + k_term + r_term[i : i + 1]).astype(BF16)

    to_next.wait_send()
    to_prev.wait_send()
    to_mate.wait_send()
    remote(send1.at[pl.ds(0, 31)], recv1.at[pl.ds(0, 31)], s_1, r_1, mate).wait_send()
    remote(tok_recv.at[pl.ds(0, 63)], tok_recv.at[pl.ds(0, 63)], s_t, r_t, mate).wait_send()
    remote(send3.at[pl.ds(0, 31)], recv3.at[pl.ds(0, 31)], s_3, r_3, mate).wait_send()
    remote(k_recv.at[pl.ds(0, 15)], k_recv.at[pl.ds(0, 15)], s_k, r_k, mate).wait_send()
    for part in range(2):
        for step in range(1, 4):
            pass_right(part, step).wait_send()

        @pl.when(jnp.logical_not(own_right))
        def _():
            pass_right(part, 0).wait_send()

    @pl.when(own_right)
    def _():
        remote(r_send, r_recv, s_r, r_r, mate).wait_send()


def store(pair_in, atoms_in, pair_to, atoms_to, done):
    first = pltpu.make_async_copy(pair_in, pair_to, done.at[0])
    second = pltpu.make_async_copy(atoms_in, atoms_to, done.at[1])
    first.start()
    second.start()
    first.wait()
    second.wait()


def per_device(
    pair, atoms, atom_token, tri_proj, tri_out, w_qkv, w_attn_out, w_token, w_row, w_col
):
    vmem = pl.BlockSpec(memory_space=pltpu.VMEM)
    sem = pltpu.SemaphoreType.DMA
    arguments = (
        pair, atoms, atom_token.reshape(1, 128), tri_proj, tri_out, w_qkv, w_attn_out, w_token,
        w_row, w_col,
    )
    results = pl.pallas_call(
        kernel,
        out_shape=(pltpu.VMEM(pair.shape, BF16), pltpu.VMEM(atoms.shape, BF16)),
        in_specs=[pl.BlockSpec(memory_space=pltpu.HBM)] * 10,
        out_specs=(vmem, vmem),
        scratch_shapes=[
            pltpu.VMEM(pair.shape, BF16),
            pltpu.VMEM(atoms.shape, BF16),
            pltpu.VMEM((1, 128), jnp.int32),
            pltpu.VMEM(tri_proj.shape, BF16),
            pltpu.VMEM(tri_out.shape, BF16),
            pltpu.VMEM(w_qkv.shape, BF16),
            pltpu.VMEM(w_attn_out.shape, BF16),
            pltpu.VMEM(w_token.shape, BF16),
            pltpu.VMEM(w_row.shape, BF16),
            pltpu.VMEM(w_col.shape, BF16),
            pltpu.VMEM((512, C), F32),
            pltpu.VMEM((32, 16, C), BF16),
            pltpu.VMEM((32, 16, C), BF16),
            pltpu.VMEM((2, 4, 64, C), BF16),
            pltpu.VMEM((4, 64, C), BF16),
            pltpu.VMEM((4, 4, 64, C), BF16),
            pltpu.VMEM((32, 8, C), BF16),
            pltpu.VMEM((32, 8, C), BF16),
            pltpu.VMEM((256, C), F32),
            pltpu.VMEM((256, C), F32),
            pltpu.VMEM((48, C), BF16),
            pltpu.VMEM((48, C), BF16),
            pltpu.VMEM((2, 16, 16, C), BF16),
            pltpu.VMEM((64, 16, C), BF16),
            pltpu.VMEM((8, C), F32),
            pltpu.VMEM((16, 8, C), F32),
            pltpu.VMEM((8, C), F32),
            pltpu.VMEM((8, C), F32),
            sem((2,)), sem((2,)),
            sem, sem,
            sem((8,)), sem((8,)),
            sem, sem,
            sem, sem,
            sem, sem,
            sem, sem,
            sem, sem,
            sem((10,)),
            pltpu.SemaphoreType.REGULAR,
        ],
        compiler_params=pltpu.CompilerParams(
            collective_id=0, has_side_effects=True, vmem_limit_bytes=32 << 20
        ),
    )(*(pltpu.with_memory_space_constraint(value, pltpu.HBM) for value in arguments))
    hbm = pl.BlockSpec(memory_space=pltpu.HBM)
    return pl.pallas_call(
        store,
        out_shape=(
            jax.ShapeDtypeStruct(pair.shape, BF16),
            jax.ShapeDtypeStruct(atoms.shape, BF16),
        ),
        in_specs=[vmem, vmem],
        out_specs=(hbm, hbm),
        scratch_shapes=[sem((2,))],
    )(*(pltpu.with_memory_space_constraint(value, pltpu.VMEM) for value in results))


def solution(mesh):
    return jax.shard_map(
        per_device,
        mesh=mesh,
        in_specs=(
            P("row", "col", None),
            P("row", None),
            P("row"),
            P(),
            P(),
            P(),
            P(),
            P(),
            P(),
            P(),
        ),
        out_specs=(P("row", "col", None), P("row", None)),
        check_vma=False,
    )
```

time: 33.2 us -> 33.3 us (level)
  the two profiles are of different devices: /device:TPU:4 before, /device:TPU:1 now
where the time goes in v4:
time: 33.3 us; the launch traced here: 33.2 us
  Pallas kernels  32.6 us (98%)
  between operations  0.64 us (2%)
    pallas_call x1, Pallas kernels, per_device(): pl.pallas_call(kernel, out_shape=(pltpu.VMEM(pair.shape, BF16), pltpu.VME...  31.9 us

profile of v4, /device:TPU:1, one launch (start us, length us, event | category | flops | bytes accessed | tf_op | source)
XLA Modules:
  0.0 33.2 jit_solution(10996305062927708775)
XLA Ops:
  0.6 31.9 %shard_map.113 = (bf16[4,64,128]{2,1,0:T(8,128)(2,1)S(1)}, bf16[128,128]{1,0:T(8,128)(2,1)S(1)}) custom-call(bf16[4,64,128]{2,1,0:T(8,128)(2,1)} %pair_in.1, bf16[128,128]{1,0:T(8,128)(2,1)} %atoms_in.1, s32[1,128]{1,0:T(1,128)} %bitcast.1, bf16[128,640]{1,0:T(8,128)(2,1)} %tri_proj_in.1, bf16[128,128]{1,0:T(8,128)(2,1)} %tri_out_in.1, ...), custom_call_target="tpu_custom_call" | custom-call | tf_op jit(solution)/shard_map/pallas_call | solution.py:391
  32.6 0.7 %shard_map.114 = (bf16[4,64,128]{2,1,0:T(8,128)(2,1)}, bf16[128,128]{1,0:T(8,128)(2,1)}) custom-call(bf16[4,64,128]{2,1,0:T(8,128)(2,1)S(1)} %get-tuple-element.4.pair_in, bf16[128,128]{1,0:T(8,128)(2,1)S(1)} %get-tuple-element.5.atoms_in), custom_call_target="tpu_custom_call" | custom-call | tf_op jit(solution)/shard_map/pallas_call | solution.py:441

commit v5 on v4

--- a/solution.py
+++ b/solution.py
@@ -46,7 +46,7 @@
     pair_ref, atoms_ref, token_ref, tri_proj_ref, tri_out_ref, w_qkv_ref, w_attn_ref, w_token_ref,
     w_row_ref, w_col_ref,
     wide, send1, recv1, left, right, rights, send3, recv3, gate_ref, upd_ref,
-    before, after, tok_send, tok_recv, k_send, k_recv, r_send, r_recv,
+    before, after, token_before, token_after, tok_send, tok_recv, k_send, k_recv, r_recv,
     s_halo, r_halo, s_1, r_1, s_2, r_2, s_l, r_l, s_3, r_3, s_t, r_t, s_k, r_k, s_r, r_r,
     s_in, plane_in,
 ):
@@ -173,12 +173,17 @@
     arguments[2].wait()
     to_next = remote(atoms_ref.at[pl.ds(80, 48)], before, s_halo.at[0], r_halo.at[0], next_row())
     to_prev = remote(atoms_ref.at[pl.ds(0, 48)], after, s_halo.at[1], r_halo.at[1], prev_row())
+    arguments[6].wait()
+    ids_next = remote(token_ref, token_before, s_halo.at[2], r_halo.at[2], next_row())
+    ids_prev = remote(token_ref, token_after, s_halo.at[3], r_halo.at[3], prev_row())
     to_next.start()
     to_prev.start()
+    ids_next.start()
+    ids_prev.start()
 
     plane(lambda group_to, to: remote(send1.at[group_to], recv1.at[group], s_1, r_1, to).start())
 
-    for k in range(3, 10):
+    for k in (3, 4, 5, 7, 8, 9):
         arguments[k].wait()
     atoms = atoms_ref[...].astype(F32)
     own = dot(normed(atoms).astype(BF16), w_qkv_ref[...]).astype(BF16)
@@ -188,12 +193,19 @@
     picked = jnp.where(token_id == token_ref[...], 1.0, 0.0).astype(BF16)
     to_next.wait_recv()
     to_prev.wait_recv()
+    ids_next.wait_recv()
+    ids_prev.wait_recv()
+    count = picked.astype(F32)
+    for ids in (token_before, token_after):
+        count = count + jnp.where(token_id == ids[...], 1.0, 0.0)
+    count = jnp.maximum(jnp.sum(count, axis=1, keepdims=True), 1.0)
     edge = jnp.concatenate([before[...], after[...]], axis=0).astype(F32)
     edge = dot(normed(edge).astype(BF16), w_qkv_ref[:, C:]).astype(BF16)
     keys = jnp.concatenate([edge[0:48, :C], own[:, C : 2 * C], edge[48:96, :C]], axis=0)
     values = jnp.concatenate([edge[0:48, C:], own[:, 2 * C :], edge[48:96, C:]], axis=0)
     head_of = lax.broadcasted_iota(jnp.int32, (32, C), 1) // 32
     attended = []
+    ones = jnp.ones((128, C), BF16)
     for window in range(4):
         at = 32 * window
         query = own[at : at + 32, :C]
@@ -204,8 +216,8 @@
         position = row * 128 + at - 48 + lax.broadcasted_iota(jnp.int32, (128, 128), 1)
         scores = jnp.where((position >= 0) & (position < 8192), scores, -1e30)
         probs = jnp.exp(scores - jnp.max(scores, axis=-1, keepdims=True))
-        probs = (probs / jnp.sum(probs, axis=-1, keepdims=True)).astype(BF16)
-        mixed = dot(probs, values[at : at + 128])
+        mixed = dot(probs.astype(BF16), jnp.concatenate([values[at : at + 128], ones], axis=1))
+        mixed = mixed[:, :C] / mixed[:, C:]
         result = mixed[0:32]
         for h in range(1, HEADS):
             result = jnp.where(head_of == h, mixed[32 * h : 32 * h + 32], result)
@@ -246,23 +258,20 @@
     atom_out = (atoms + dot(attended, w_attn_ref[...])).astype(BF16)
     atom_out_ref[...] = atom_out
     hidden = jnp.maximum(dot(atom_out, w_token_ref[...]), 0.0).astype(BF16)
-    summed = dot(picked, hidden).astype(BF16)
-    count = jnp.broadcast_to(jnp.sum(picked.astype(F32), axis=1, keepdims=True), (128, C))
-    count = jnp.where(lane < 64, pltpu.roll(count.reshape(16, 8, C), 4, 1).reshape(128, C), count)
-    k_part = dot(summed, w_col_ref[...])
-    r_part = dot(summed, w_row_ref[...])
-    r_swap = pltpu.roll(r_part.reshape(16, 8, C), 4, 1).reshape(128, C)
-    for high, part in ((0, r_part), (1, r_swap)):
-        part = jnp.where(line % 8 < 4, part, count)
-        tok_send[high] = jnp.concatenate(
-            [k_part.reshape(16, 8, C), part.reshape(16, 8, C)], axis=1
-        ).astype(BF16)
-    tok_recv[pl.ds(row, 1)] = tok_send[pl.ds(x // 2, 1), pl.ds(p, 1)].reshape(1, 16, C)
+    single = (dot(picked, hidden) / count).astype(BF16)
+    k_part = dot(single, w_col_ref[...])
+    r_part = dot(single, w_row_ref[...])
+    k_swap, r_swap = (pltpu.roll(part.reshape(16, 8, C), 4, 1).reshape(128, C) for part in (k_part, r_part))
+    for k_high in range(2):
+        for r_high in range(2):
+            part = jnp.where(line % 8 < 4, (k_part, k_swap)[k_high], (r_swap, r_part)[r_high])
+            tok_send[k_high, r_high] = part.reshape(16, 8, C).astype(BF16)
+    tok_recv[pl.ds(row, 1)] = tok_send[pl.ds(z_hi, 1), pl.ds(x // 2, 1), pl.ds(p, 1)].reshape(1, 8, C)
 
     pl.semaphore_wait(plane_in, 3)
 
     def give(x_to, piece, to):
-        remote(tok_send.at[x_to // 2, piece], tok_recv.at[row], s_t, r_t, to).start()
+        remote(tok_send.at[to[1] // 2, x_to // 2, piece], tok_recv.at[row], s_t, r_t, to).start()
 
     other_x(give, (2, 7, 1, 0))
     same_x(give, (2, 7, 1, 0))
@@ -304,22 +313,18 @@
     plane(lambda group_to, to: remote(send3.at[group_to], recv3.at[group], s_3, r_3, to).start())
 
     remote(tok_recv.at[pl.ds(0, 63)], tok_recv.at[pl.ds(0, 63)], s_t, r_t, mate).wait_recv()
-    total = jnp.sum(tok_recv[...].astype(F32), axis=0)
-    count = total[8:16]
-    swap = pltpu.roll(count, 64, 1)
-    lane, line = lane[0:8], line[0:8]
-    low = pltpu.roll(jnp.where(lane < 64, count, swap), 4, 0)
-    high = jnp.where(lane < 64, swap, count)
-    k_send[...] = total[0:8] / jnp.where(line < 4, low, high)
+    k_send[...] = jnp.sum(tok_recv[...].astype(F32), axis=0)
     k_recv[pl.ds(p, 1)] = k_send[...][None]
-    same_x(lambda x_to, piece, to: remote(k_send, k_recv.at[p], s_k, r_k, to).start(), (2, 7, 1, 0))
-    count = jnp.where(x // 2 == 0, low, pltpu.roll(high, 4, 0))
-    r_send[...] = total[8:16] / jnp.where(line < 4, count, 1.0)
+    for z_step in (3, 2, 1, 0):
+        z_to = z_hi * 4 + (z_lo + z_step) % 4
+        for step in (2, 1, 3, 0):
+            if step or z_step:
+                remote(k_send, k_recv.at[p], s_k, r_k, place_of(x, ys[step], z_to)).start()
 
     @pl.when(own_right)
     def _():
-        r_recv[...] = r_send[...]
-        remote(r_send, r_recv, s_r, r_r, mate).start()
+        r_recv[...] = k_send[...]
+        remote(k_send, r_recv, s_r, r_r, mate).start()
 
     remote(send3.at[pl.ds(0, 31)], recv3.at[pl.ds(0, 31)], s_3, r_3, mate).wait_recv()
     wide[0:256, :] = recv3[...].reshape(256, C).astype(F32)
@@ -342,14 +347,16 @@
 
     @pl.when(jnp.logical_not(own_right))
     def _():
-        remote(r_send, r_recv, s_r, r_r, mate).wait_recv()
+        remote(k_send, r_recv, s_r, r_r, mate).wait_recv()
 
     k_term = k_recv[...]
-    k_term = jnp.where(z_hi == 0, k_term[:, 0:4], k_term[:, 4:8]).reshape(64, C)
-    r_term = r_recv[...]
+    k_term = k_term[:, 0:4].reshape(64, C)
+    r_term = r_recv[4:8, :]
     for i in range(4):
         pair_out_ref[i] = (update[i * 64 : i * 64 + 64] + k_term + r_term[i : i + 1]).astype(BF16)
 
+    ids_next.wait_send()
+    ids_prev.wait_send()
     to_next.wait_send()
     to_prev.wait_send()
     to_mate.wait_send()
@@ -367,7 +374,7 @@
 
     @pl.when(own_right)
     def _():
-        remote(r_send, r_recv, s_r, r_r, mate).wait_send()
+        remote(k_send, r_recv, s_r, r_r, mate).wait_send()
 
 
 def store(pair_in, atoms_in, pair_to, atoms_to, done):
@@ -416,13 +423,14 @@
             pltpu.VMEM((256, C), F32),
             pltpu.VMEM((48, C), BF16),
             pltpu.VMEM((48, C), BF16),
-            pltpu.VMEM((2, 16, 16, C), BF16),
-            pltpu.VMEM((64, 16, C), BF16),
+            pltpu.VMEM((1, 128), jnp.int32),
+            pltpu.VMEM((1, 128), jnp.int32),
+            pltpu.VMEM((2, 2, 16, 8, C), BF16),
+            pltpu.VMEM((64, 8, C), BF16),
             pltpu.VMEM((8, C), F32),
             pltpu.VMEM((16, 8, C), F32),
             pltpu.VMEM((8, C), F32),
-            pltpu.VMEM((8, C), F32),
-            sem((2,)), sem((2,)),
+            sem((4,)), sem((4,)),
             sem, sem,
             sem((8,)), sem((8,)),
             sem, sem,

time: 33.3 us -> 31.5 us (0.946)
  Pallas kernels: 32.6 us -> 30.7 us
    pallas_call x1, Pallas kernels: 31.9 us -> 30.1 us  [per_device(): pl.pallas_call(kernel, out_shape=(pltpu.VMEM(pair.shape, BF16), pltpu.VME...]
where the time goes in v5:
time: 31.5 us; the launch traced here: 31.4 us
  Pallas kernels  30.7 us (97%)
  between operations  0.64 us (2%)
    pallas_call x1, Pallas kernels, per_device(): pl.pallas_call(kernel, out_shape=(pltpu.VMEM(pair.shape, BF16), pltpu.VME...  30.1 us
    pallas_call x1, Pallas kernels, per_device(): pl.pallas_call(store, out_shape=(jax.ShapeDtypeStruct(pair.shape, BF16),...  0.66 us

profile of v5, /device:TPU:1, one launch (start us, length us, event | category | flops | bytes accessed | tf_op | source)
XLA Modules:
  0.0 31.4 jit_solution(15031865364535876065)
XLA Ops:
  0.6 30.1 %shard_map.113 = (bf16[4,64,128]{2,1,0:T(8,128)(2,1)S(1)}, bf16[128,128]{1,0:T(8,128)(2,1)S(1)}) custom-call(bf16[4,64,128]{2,1,0:T(8,128)(2,1)} %pair_in.1, bf16[128,128]{1,0:T(8,128)(2,1)} %atoms_in.1, s32[1,128]{1,0:T(1,128)} %bitcast.1, bf16[128,640]{1,0:T(8,128)(2,1)} %tri_proj_in.1, bf16[128,128]{1,0:T(8,128)(2,1)} %tri_out_in.1, ...), custom_call_target="tpu_custom_call" | custom-call | tf_op jit(solution)/shard_map/pallas_call | solution.py:398
  30.7 0.7 %shard_map.114 = (bf16[4,64,128]{2,1,0:T(8,128)(2,1)}, bf16[128,128]{1,0:T(8,128)(2,1)}) custom-call(bf16[4,64,128]{2,1,0:T(8,128)(2,1)S(1)} %get-tuple-element.4.pair_in, bf16[128,128]{1,0:T(8,128)(2,1)S(1)} %get-tuple-element.5.atoms_in), custom_call_target="tpu_custom_call" | custom-call | tf_op jit(solution)/shard_map/pallas_call | solution.py:449

commit v6 on v5

--- a/solution.py
+++ b/solution.py
@@ -31,6 +31,10 @@
 
 def dot_nt(a, b):
     return lax.dot_general(a, b, (((1,), (1,)), ((), ())), preferred_element_type=F32)
+
+
+def dot_tn(a, b):
+    return lax.dot_general(a, b, (((0,), (0,)), ((), ())), preferred_element_type=F32)
 
 
 def halves(low, high):
@@ -131,8 +135,6 @@
             )
         )
     ]
-    for k in range(3):
-        arguments[k].start()
 
     barrier = pltpu.get_barrier_semaphore()
 
@@ -147,7 +149,7 @@
     hello(prev_row())
     hello(mate)
 
-    for k in range(3, 10):
+    for k in range(10):
         arguments[k].start()
 
     arguments[0].wait()
@@ -212,11 +214,11 @@
         query = jnp.concatenate(
             [jnp.where(head_of == h, query, jnp.zeros_like(query)) for h in range(HEADS)], axis=0
         )
-        scores = dot_nt(query, keys[at : at + 128]) * (32.0**-0.5)
-        position = row * 128 + at - 48 + lax.broadcasted_iota(jnp.int32, (128, 128), 1)
+        scores = dot_nt(keys[at : at + 128], query) * (32.0**-0.5)
+        position = row * 128 + at - 48 + line
         scores = jnp.where((position >= 0) & (position < 8192), scores, -1e30)
-        probs = jnp.exp(scores - jnp.max(scores, axis=-1, keepdims=True))
-        mixed = dot(probs.astype(BF16), jnp.concatenate([values[at : at + 128], ones], axis=1))
+        probs = jnp.exp(scores - jnp.max(scores, axis=0, keepdims=True))
+        mixed = dot_tn(probs.astype(BF16), jnp.concatenate([values[at : at + 128], ones], axis=1))
         mixed = mixed[:, :C] / mixed[:, C:]
         result = mixed[0:32]
         for h in range(1, HEADS):
@@ -241,13 +243,12 @@
 
     def pass_right(part, step):
         return remote(
-            right.at[pl.ds(2 * part, 2)], rights.at[place, pl.ds(2 * part, 2)],
-            s_2.at[2 * step + part], r_2.at[2 * place + part], along_x(step, parity),
-        )
-
-    for part in range(2):
-        assemble(1, 2 * part)
-        assemble(1, 2 * part + 1)
+            right.at[part], rights.at[place, part],
+            s_2.at[4 * step + part], r_2.at[4 * place + part], along_x(step, parity),
+        )
+
+    for part in range(4):
+        assemble(1, part)
         for step in (2, 1, 3):
             pass_right(part, step).start()
 
@@ -287,15 +288,13 @@
 
     remote(left.at[1 - core], left.at[1 - core], s_l, r_l, mate).wait_recv()
     for slot in range(4):
-        if slot % 2 == 0:
-            for source in range(4):
-
-                @pl.when(jnp.logical_not(own_right & (place == source)))
-                def _():
-                    remote(
-                        right.at[pl.ds(slot, 2)], rights.at[source, pl.ds(slot, 2)],
-                        s_2.at[0], r_2.at[2 * source + slot // 2], mate,
-                    ).wait_recv()
+        for source in range(4):
+
+            @pl.when(jnp.logical_not(own_right & (place == source)))
+            def _():
+                remote(
+                    right.at[slot], rights.at[source, slot], s_2.at[0], r_2.at[4 * source + slot], mate
+                ).wait_recv()
 
         tri = None
         for k in range(2):
@@ -313,7 +312,7 @@
     plane(lambda group_to, to: remote(send3.at[group_to], recv3.at[group], s_3, r_3, to).start())
 
     remote(tok_recv.at[pl.ds(0, 63)], tok_recv.at[pl.ds(0, 63)], s_t, r_t, mate).wait_recv()
-    k_send[...] = jnp.sum(tok_recv[...].astype(F32), axis=0)
+    k_send[...] = jnp.sum(tok_recv[...].astype(F32), axis=0).astype(BF16)
     k_recv[pl.ds(p, 1)] = k_send[...][None]
     for z_step in (3, 2, 1, 0):
         z_to = z_hi * 4 + (z_lo + z_step) % 4
@@ -349,9 +348,9 @@
     def _():
         remote(k_send, r_recv, s_r, r_r, mate).wait_recv()
 
-    k_term = k_recv[...]
+    k_term = k_recv[...].astype(F32)
     k_term = k_term[:, 0:4].reshape(64, C)
-    r_term = r_recv[4:8, :]
+    r_term = r_recv[...].astype(F32)[4:8]
     for i in range(4):
         pair_out_ref[i] = (update[i * 64 : i * 64 + 64] + k_term + r_term[i : i + 1]).astype(BF16)
 
@@ -364,7 +363,7 @@
     remote(tok_recv.at[pl.ds(0, 63)], tok_recv.at[pl.ds(0, 63)], s_t, r_t, mate).wait_send()
     remote(send3.at[pl.ds(0, 31)], recv3.at[pl.ds(0, 31)], s_3, r_3, mate).wait_send()
     remote(k_recv.at[pl.ds(0, 15)], k_recv.at[pl.ds(0, 15)], s_k, r_k, mate).wait_send()
-    for part in range(2):
+    for part in range(4):
         for step in range(1, 4):
             pass_right(part, step).wait_send()
 
@@ -427,12 +426,12 @@
             pltpu.VMEM((1, 128), jnp.int32),
             pltpu.VMEM((2, 2, 16, 8, C), BF16),
             pltpu.VMEM((64, 8, C), BF16),
-            pltpu.VMEM((8, C), F32),
-            pltpu.VMEM((16, 8, C), F32),
-            pltpu.VMEM((8, C), F32),
+            pltpu.VMEM((8, C), BF16),
+            pltpu.VMEM((16, 8, C), BF16),
+            pltpu.VMEM((8, C), BF16),
             sem((4,)), sem((4,)),
             sem, sem,
-            sem((8,)), sem((8,)),
+            sem((16,)), sem((16,)),
             sem, sem,
             sem, sem,
             sem, sem,

time: 31.5 us -> 31.5 us (level)
  no operation moved by 1% of the time
where the time goes in v6:
time: 31.5 us; the launch traced here: 31.4 us
  Pallas kernels  30.7 us (97%)
  between operations  0.64 us (2%)
    pallas_call x1, Pallas kernels, per_device(): pl.pallas_call(kernel, out_shape=(pltpu.VMEM(pair.shape, BF16), pltpu.VME...  30.1 us
    pallas_call x1, Pallas kernels, per_device(): pl.pallas_call(store, out_shape=(jax.ShapeDtypeStruct(pair.shape, BF16),...  0.66 us

profile of v6, /device:TPU:1, one launch (start us, length us, event | category | flops | bytes accessed | tf_op | source)
XLA Modules:
  0.0 31.4 jit_solution(9899842052205601605)
XLA Ops:
  0.6 30.1 %shard_map.113 = (bf16[4,64,128]{2,1,0:T(8,128)(2,1)S(1)}, bf16[128,128]{1,0:T(8,128)(2,1)S(1)}) custom-call(bf16[4,64,128]{2,1,0:T(8,128)(2,1)} %pair_in.1, bf16[128,128]{1,0:T(8,128)(2,1)} %atoms_in.1, s32[1,128]{1,0:T(1,128)} %bitcast.1, bf16[128,640]{1,0:T(8,128)(2,1)} %tri_proj_in.1, bf16[128,128]{1,0:T(8,128)(2,1)} %tri_out_in.1, ...), custom_call_target="tpu_custom_call" | custom-call | tf_op jit(solution)/shard_map/pallas_call | solution.py:397
  30.7 0.7 %shard_map.114 = (bf16[4,64,128]{2,1,0:T(8,128)(2,1)}, bf16[128,128]{1,0:T(8,128)(2,1)}) custom-call(bf16[4,64,128]{2,1,0:T(8,128)(2,1)S(1)} %get-tuple-element.4.pair_in, bf16[128,128]{1,0:T(8,128)(2,1)S(1)} %get-tuple-element.5.atoms_in), custom_call_target="tpu_custom_call" | custom-call | tf_op jit(solution)/shard_map/pallas_call | solution.py:448

commit v7 on v6

--- a/solution.py
+++ b/solution.py
@@ -333,8 +333,8 @@
         )
         centered = tri - jnp.mean(tri, axis=0, keepdims=True)
         variance = jnp.mean(centered * centered, axis=0, keepdims=True)
-        tri_norm = (centered * lax.rsqrt(variance + 1e-05)).T.astype(BF16)
-        update = dot(tri_norm, tri_out_ref[...])
+        tri_norm = (centered * lax.rsqrt(variance + 1e-05)).astype(BF16)
+        update = dot_tn(tri_norm, tri_out_ref[...])
         for odd in range(2):
             for i in range(4):
                 upd_ref[pl.ds((half * 2 + odd) * 64 + i, 16, stride=4), :] = update[

time: 31.5 us -> 31.4 us (level)
  no operation moved by 1% of the time
where the time goes in v7:
time: 31.4 us; the launch traced here: 31.3 us
  Pallas kernels  30.7 us (98%)
  between operations  0.64 us (2%)
    pallas_call x1, Pallas kernels, per_device(): pl.pallas_call(kernel, out_shape=(pltpu.VMEM(pair.shape, BF16), pltpu.VME...  30 us
    pallas_call x1, Pallas kernels, per_device(): pl.pallas_call(store, out_shape=(jax.ShapeDtypeStruct(pair.shape, BF16),...  0.66 us

profile of v7, /device:TPU:1, one launch (start us, length us, event | category | flops | bytes accessed | tf_op | source)
XLA Modules:
  0.0 31.3 jit_solution(13374883469574679161)
XLA Ops:
  0.6 30.0 %shard_map.113 = (bf16[4,64,128]{2,1,0:T(8,128)(2,1)S(1)}, bf16[128,128]{1,0:T(8,128)(2,1)S(1)}) custom-call(bf16[4,64,128]{2,1,0:T(8,128)(2,1)} %pair_in.1, bf16[128,128]{1,0:T(8,128)(2,1)} %atoms_in.1, s32[1,128]{1,0:T(1,128)} %bitcast.1, bf16[128,640]{1,0:T(8,128)(2,1)} %tri_proj_in.1, bf16[128,128]{1,0:T(8,128)(2,1)} %tri_out_in.1, ...), custom_call_target="tpu_custom_call" | custom-call | tf_op jit(solution)/shard_map/pallas_call | solution.py:397
  30.7 0.7 %shard_map.114 = (bf16[4,64,128]{2,1,0:T(8,128)(2,1)}, bf16[128,128]{1,0:T(8,128)(2,1)}) custom-call(bf16[4,64,128]{2,1,0:T(8,128)(2,1)S(1)} %get-tuple-element.4.pair_in, bf16[128,128]{1,0:T(8,128)(2,1)S(1)} %get-tuple-element.5.atoms_in), custom_call_target="tpu_custom_call" | custom-call | tf_op jit(solution)/shard_map/pallas_call | solution.py:448
